TPU v7x, 256 devices: a whole 4x4x8 slice. The times are simulated.
256 devices in a mesh: row: 32 (over y, z), col: 8 (over x, core).
Axes of the slice: x: 4, y: 4, z: 8, core: 2. Of those that a mesh axis runs over, the one named last changes fastest.
Arguments:
- features: bfloat16 [65536, 128], P(('row', 'col')), may hold values from -6 to 6
- tiles: bfloat16 [32, 8, 128, 128, 128], P('row', 'col'), may hold values from -6 to 6
- block_rows: int32 [32, 8, 128], P('row', 'col'), may hold values from 0 to 15
- block_cols: int32 [32, 8, 128], P('row', 'col'), may hold values from 0 to 63
- labels: int32 [65536], P(('row', 'col')), may hold values from 0 to 171
- train_mask: int32 [65536], P(('row', 'col')), may hold values 0 or 1
- self_first: bfloat16 [128, 256], replicated, may hold values from -0.5 to 0.5
- neigh_first: bfloat16 [128, 256], replicated, may hold values from -0.5 to 0.5
- bias_first: float32 [256], replicated, may hold values from -4 to 4
- self_second: bfloat16 [256, 172], replicated, may hold values from -0.375 to 0.375
- neigh_second: bfloat16 [256, 172], replicated, may hold values from -0.375 to 0.375
- bias_second: float32 [172], replicated, may hold values from -4 to 4
Outputs:
- grad_self_first: float32 [128, 256], replicated
- grad_neigh_first: float32 [128, 256], replicated
- grad_bias_first: float32 [256], replicated
- grad_self_second: float32 [256, 172], replicated
- grad_neigh_second: float32 [256, 172], replicated
- grad_bias_second: float32 [172], replicated
All inputs are finite; a program needn't handle non-finite values. No bound on the sum of `train_mask` on one device may be relied on, other than what follows from the above.
Results may differ from a plain program's by a relative error of at most 0.014.
The roundings to bfloat16 on the way count: a program that leaves them out, or rounds other values in their place, can miss the bound.
Values may be sent and summed in bfloat16 or wider, within the bound.
No kernel may reach another device: no remote copies, remote signals or barrier semaphores. Data moves between devices by JAX's collectives and lax.ppermute only.
A program may use at most 128 MiB of HBM per device.

v0:
```python
import functools
import math

import jax
import jax.numpy as jnp
from jax import lax
from jax.experimental import pallas as pl
from jax.experimental.pallas import tpu as pltpu
from jax.sharding import PartitionSpec as P

EDGE = 128
GROUP = 32
PAD = 176
NY, NZ = 4, 8
F32, BF16 = jnp.float32, jnp.bfloat16
VMEM = pl.BlockSpec(memory_space=pltpu.VMEM)
SMEM = pl.BlockSpec(memory_space=pltpu.SMEM)
ANY = pl.BlockSpec(memory_space=pl.ANY)
NT = (((1,), (1,)), ((), ()))


def dot(a, b):
    return jnp.dot(a, b, preferred_element_type=F32)


def dot_nt(a, b):
    return lax.dot_general(a, b, NT, preferred_element_type=F32)


def call(body, out, specs, scratch=(), mib=4, flops=0, bytes_accessed=0):
    return pl.pallas_call(
        body,
        out_shape=out,
        in_specs=specs,
        out_specs=jax.tree.map(lambda _: VMEM, out),
        scratch_shapes=list(scratch),
        compiler_params=pltpu.CompilerParams(vmem_limit_bytes=mib * 1024 * 1024),
        cost_estimate=pl.CostEstimate(
            flops=flops, bytes_accessed=bytes_accessed, transcendentals=0
        ),
    )


def step(x, groups, shift):
    pairs = [(g[i], g[(i + shift) % len(g)]) for g in groups for i in range(len(g))]
    return lax.ppermute(x, "row", pairs)


ALONG_Z = [[NZ * y + z for z in range(NZ)] for y in range(NY)]
ALONG_Y = [[NZ * y + z for y in range(NY)] for z in range(NZ)]


def ring(x, groups):
    count = len(groups[0])
    up = down = x
    parts = [x]
    for _ in range(count // 2 - 1):
        up, down = step(up, groups, 1), step(down, groups, -1)
        parts += [up, down]
    half = x.shape[0] // 2
    return parts + [step(up[:half], groups, 1), step(down[half:], groups, -1)]


def along_y(x):
    return [x, step(x, ALONG_Y, 1), step(x, ALONG_Y, -1), step(x, ALONG_Y, 2)]


def place_of(block, row):
    owner = block // 2
    dz = (owner % NZ + NZ - row % NZ) % NZ
    dy = (owner // NZ + NY - row // NZ) % NY
    z_place = jnp.where(dz <= 3, 2 * dz, jnp.where(dz == 4, 7, 15 - 2 * dz))
    y_place = jnp.where(dy == 0, 0, jnp.where(dy == 3, 1, dy + 1))
    return z_place * NY + y_place


def slot_of(block, col):
    owner = block // 2
    dx = (owner // 2 + 4 - col // 2) % 4
    dc = (owner + col) % 2
    return (dc * 4 + dx) * 2 + block % 2


def to_sibling(x):
    return lax.ppermute(x, "col", [(i, i ^ 1) for i in range(8)])


def along_x(x, shift):
    return lax.ppermute(x, "col", [(i, (i + 2 * shift) % 8) for i in range(8)])


def start_parts(parts, held, sems):
    copies, at = [], 0
    for i, p in enumerate(parts):
        n = p.shape[0]
        copies.append(pltpu.make_async_copy(p, held.at[pl.ds(at, n)], sems.at[i]))
        copies[-1].start()
        at += n
    return copies


def start_pairs(feat_parts, agg_parts, held, sems):
    copies, at = [], 0
    for i, pair in enumerate(zip(feat_parts, agg_parts)):
        n = pair[0].shape[0]
        for j, p in enumerate(pair):
            to = held.at[pl.ds(at, n), :, pl.ds(j * EDGE, EDGE)]
            copies.append(pltpu.make_async_copy(p, to, sems.at[2 * i + j]))
            copies[-1].start()
        at += n
    return copies


def accumulate(count, product, add, group=GROUP):
    def body(i, carry):
        got = [product(i * group + u) for u in range(group)]
        for u in range(group):
            add(i * group + u, got[u])
        return carry

    lax.fori_loop(0, count // group, body, 0)


def degree_kernel(first, slots, tiles, out):
    out[...] = jnp.zeros_like(out)
    ones = jnp.ones((8, EDGE), BF16)

    def product(t):
        x = tiles[first + t].astype(F32)
        x = x * x
        hi = x.astype(BF16)
        lo = (x - hi.astype(F32)).astype(BF16)
        return dot_nt(ones, hi) + dot_nt(ones, lo)

    def add(t, got):
        out[slots[first + t]] += got

    accumulate(GROUP, product, add, 4)


def first_kernel(n_parts, offs, cols, tiles, d0, d1, d2, d3, *refs):
    parts, keep, send, held, acc, sem = refs[:n_parts], *refs[n_parts:]
    copies = start_parts(parts, held, sem)
    acc[...] = jnp.zeros_like(acc)
    for s in range(16):
        deg = (d0[s][:1] + d1[s][:1]) + (d2[s][:1] + d3[s][:1])
        acc[pl.ds(s // 2 * 264 + 256 + s % 2, 1), :] = deg
    for c in copies:
        c.wait()

    def add(t, got):
        acc[pl.ds(pl.multiple_of(offs[t], 8), EDGE), :] += got

    accumulate(tiles.shape[0], lambda t: dot(tiles[t], held[cols[t]]), add)
    keep[...] = acc[pl.ds(0, 1056), :]
    send[...] = acc[pl.ds(1056, 1056), :]


def join_first_kernel(keep, got, *out):
    for x in range(4):
        at = pl.ds(x * 264, 264)
        out[x][...] = keep[at, :] + got[at, :]


def flip(x):
    return x.astype(F32).T


def flip(x):
    return x.astype(F32).T


def aggregate_kernel(s0, s1, s2, s3, agg, inv):
    total = (s0[...] + s1[...]) + (s2[...] + s3[...])
    for b in range(2):
        x = 1.0 + total[256 + b : 257 + b]
        r = lax.rsqrt(x)
        r = r * (1.5 - 0.5 * x * r * r)
        inv[pl.ds(b, 1), :] = r
        column = jnp.broadcast_to(r, (EDGE, EDGE)).T
        agg[b] = (column * total[b * EDGE : (b + 1) * EDGE]).astype(BF16)


def second_kernel(n_parts, slots, cols, tiles, neigh, weights, bias, *refs):
    feat_parts, agg_parts = refs[:n_parts], refs[n_parts : 2 * n_parts]
    agg, keep, send, mine, held, acc = refs[2 * n_parts :]
    acc[...] = jnp.zeros_like(acc)
    weights_t = flip(weights[...]).astype(BF16)
    wide = 4
    bias_t = jnp.broadcast_to(bias[...], (wide * EDGE, bias.shape[1])).T
    first = 0
    for feat_part, agg_part in zip(feat_parts, agg_parts):

        def hidden(i, carry, feat_part=feat_part, agg_part=agg_part, first=first):
            these = pl.ds(i * wide, wide)
            x = jnp.concatenate([feat_part[these], agg_part[these]], axis=2)
            x = dot_nt(weights_t, x.reshape(wide * EDGE, 2 * EDGE)) + bias_t
            h = jnp.maximum(x, 0.0).astype(BF16)
            for q in range(wide):
                held[first + i * wide + q] = h[:, q * EDGE : (q + 1) * EDGE]
            return carry

        count = feat_part.shape[0]
        lax.fori_loop(0, count // wide, hidden, 0, unroll=True)
        first += count
    mine[...] = held[pl.ds(0, 2)]

    def add(t, got):
        acc[slots[t]] += got

    accumulate(tiles.shape[0], lambda t: dot_nt(held[cols[t]], tiles[t]), add)

    def finish(s, carry):
        for out, at in ((keep, s), (send, s + 8)):
            agg[at] = acc[at].astype(BF16)
            out[s] = dot(neigh[pl.ds(0, PAD), :], agg[at]).astype(BF16)
        return carry

    lax.fori_loop(0, 8, finish, 0)


def join_second_kernel(keep, got, *out):
    for s in range(8):
        out[s // 2][s % 2] = (keep[s].astype(F32) + got[s].astype(F32)).astype(BF16)


def loss_kernel(
    classes, scale, s0, s1, s2, s3, hid, self_t, bias, labels, mask, inv, lg, w, grad, grad_bias
):
    rows = lax.broadcasted_iota(jnp.int32, (PAD, EDGE), 0)
    ones = jnp.ones((8, EDGE), BF16)
    for b in range(2):
        total = (s0[b].astype(F32) + s1[b].astype(F32)) + (s2[b].astype(F32) + s3[b].astype(F32))
        factor = inv[b : b + 1]
        logits = dot(self_t[pl.ds(0, PAD), :], hid[b]) + factor * total + bias[...]
        logits = jnp.where(rows < classes, logits, -1e30)
        e = jnp.exp(logits - jnp.max(logits, axis=0, keepdims=True))
        p = e / jnp.sum(e, axis=0, keepdims=True)
        p = p - jnp.where(rows == labels[b : b + 1], 1.0, 0.0)
        got = (p * (mask[b : b + 1].astype(F32) * scale)).astype(BF16)
        lg[b] = got
        w[b] = (got.astype(F32) * factor).astype(BF16)
        if b == 0:
            grad[...] = dot_nt(got, hid[b])
            grad_bias[...] = dot_nt(ones, got)
        else:
            grad[...] += dot_nt(got, hid[b])
            grad_bias[...] += dot_nt(ones, got)


X_ORDER = (0, 3, 1, 2)


def last_kernel(
    n_parts, slots, cols, w0, w1, w2, w3, sibling, held, tiles, agg_second, lg, self_t, neigh_t,
    grad_self, grad_bias, *refs
):
    feat_parts, agg_parts = refs[:n_parts], refs[n_parts : 2 * n_parts]
    out, both, acc, proj, both_sem = refs[2 * n_parts :]
    copies = start_pairs(feat_parts, agg_parts, both, both_sem)
    acc[...] = jnp.zeros_like(acc)
    lacking = jnp.zeros((256 - PAD, EDGE), BF16)
    self_second = flip(self_t[...]).astype(BF16)
    neigh_second = flip(neigh_t[...]).astype(BF16)
    for b in range(2):
        acc[b] = dot(self_second, jnp.concatenate([lg[b], lacking], axis=0))
    g_neigh = jnp.zeros((PAD, 256), F32)
    for i, (dx, part) in enumerate(zip(X_ORDER, (w0, w1, w2, w3))):
        at = [(j // 2 * 4 + dx) * 2 + j % 2 for j in range(4)]
        w = jnp.concatenate([part[0], part[1], sibling[2 * i], sibling[2 * i + 1]], axis=1)
        tall = jnp.concatenate([w, jnp.concatenate([lacking] * 4, axis=1)], axis=0)
        got = dot(neigh_second, tall).astype(BF16)
        for j in range(4):
            proj[at[j]] = got[:, j * EDGE : (j + 1) * EDGE]
        g_neigh += dot_nt(w, jnp.concatenate([agg_second[s] for s in at], axis=1))
    for i in range(2):
        lanes = slice(i * EDGE, (i + 1) * EDGE)
        out[pl.ds(512 + i * PAD, PAD), :] = grad_self[:, lanes].astype(BF16)
        out[pl.ds(512 + (2 + i) * PAD, PAD), :] = g_neigh[:, lanes].astype(BF16)

    def add(t, got):
        acc[cols[t]] += got

    accumulate(tiles.shape[0], lambda t: dot(proj[slots[t]], tiles[t]), add)
    for c in copies:
        c.wait()
    wide = 8
    ones = jnp.ones((8, wide * EDGE), BF16)

    def contract(i, carry):
        g_first, g_bias = carry
        x = both[pl.ds(i * wide, wide)].reshape(wide * EDGE, 2 * EDGE)
        p = []
        for q in range(wide):
            s = i * wide + q
            p.append(jnp.where(held[s] > 0, acc[s].astype(BF16), jnp.zeros((), BF16)))
        p = jnp.concatenate(p, axis=1)
        return g_first + dot(p, x), g_bias + dot_nt(ones, p)

    zeros = (jnp.zeros((256, 256), F32), jnp.zeros((8, 256), F32))
    g_first, g_bias = lax.fori_loop(0, 64 // wide, contract, zeros)
    out[pl.ds(0, 256), :] = g_first[:, :EDGE].astype(BF16)
    out[pl.ds(256, 256), :] = g_first[:, EDGE:].astype(BF16)
    pick = lax.broadcasted_iota(jnp.int32, (16, EDGE), 0)
    second = jnp.concatenate([grad_bias[:1], jnp.zeros((1, 256 - PAD), F32)], axis=1)
    rows = (g_bias[:1, :EDGE], g_bias[:1, EDGE:], second[:, :EDGE], second[:, EDGE:])
    last = jnp.zeros((16, EDGE), F32)
    for i, row in enumerate(rows):
        last = jnp.where(pick == i, row, last)
    end = 512 + 4 * PAD
    out[pl.ds(end, 16), :] = last.astype(BF16)
    out[pl.ds(end + 16, 1280 - 16 - end), :] = jnp.zeros((1280 - 16 - end, EDGE), BF16)


def add_pieces_kernel(x, out):
    total = x[0].astype(F32)
    for i in range(1, x.shape[0]):
        total = total + x[i].astype(F32)
    out[...] = total.astype(BF16)


def add_arrays_kernel(a, b, c, d, out):
    total = (a[...].astype(F32) + b[...].astype(F32)) + (c[...].astype(F32) + d[...].astype(F32))
    out[...] = total.astype(BF16)


def spread_kernel(a, b, c, d, out):
    total = (a[...].astype(F32) + b[...].astype(F32)) + (c[...].astype(F32) + d[...].astype(F32))
    for i in range(out.shape[0]):
        out[i] = total.astype(BF16)


def unpack_kernel(classes, x, self_first, neigh_first, bias_first, self_t, neigh_t, bias_second):
    self_first[...] = flip(x[pl.ds(0, 256), :])
    neigh_first[...] = flip(x[pl.ds(256, 256), :])
    for at, out in ((512, self_t), (512 + 2 * PAD, neigh_t)):
        for i in range(2):
            got = x[pl.ds(at + i * PAD, PAD), :].astype(F32)
            out[:, i * EDGE : (i + 1) * EDGE] = got[:classes]
    last = x[pl.ds(512 + 4 * PAD, 16), :].astype(F32)
    bias_first[...] = jnp.concatenate([last[0:1], last[1:2]], axis=1)
    bias_second[...] = jnp.concatenate([last[2:3], last[3:4]], axis=1)


def sum_everywhere(x):
    every = ("row", "col")
    number = lambda y, z, x, c: ((y * NZ + z) * 4 + x) * 2 + c
    groups = [
        [number(y, z, x, c) for y in range(NY) for x in range(4)] for z in range(NZ) for c in range(2)
    ]
    x = x.reshape(16, -1, EDGE)
    piece = jax.ShapeDtypeStruct(x.shape[1:], BF16)
    x = lax.all_to_all(x, every, 0, 0, tiled=True, axis_index_groups=groups)
    x = call(add_pieces_kernel, piece, [VMEM])(x)
    near = [lax.ppermute(x, every, [(i, i ^ flip_bits) for i in range(256)]) for flip_bits in (1, 8, 9)]
    x = call(add_arrays_kernel, piece, [VMEM] * 4)(x, *near)
    far = [lax.ppermute(x, "row", [(i, i ^ flip_bits) for i in range(32)]) for flip_bits in (2, 6, 4)]
    x = call(spread_kernel, jax.ShapeDtypeStruct((16, 80, EDGE), BF16), [VMEM] * 4)(x, *far)
    x = lax.all_to_all(x, every, 0, 0, tiled=True, axis_index_groups=groups)
    return x.reshape(-1, EDGE)


def on_device(
    features,
    tiles,
    block_rows,
    block_cols,
    labels,
    train_mask,
    self_first,
    neigh_first,
    bias_first,
    self_second,
    neigh_second,
    bias_second,
):
    classes = self_second.shape[1]
    hid_size = self_first.shape[1]
    scale = 1.0 / math.sqrt(65536)
    row, col = lax.axis_index("row"), lax.axis_index("col")
    tiles = tiles.reshape(-1, EDGE, EDGE)
    slots = slot_of(block_rows.reshape(-1), col)
    sources = block_cols.reshape(-1)
    cols = place_of(sources, row) * 2 + sources % 2
    offs = slots // 2 * 264 + slots % 2 * EDGE
    shape = jax.ShapeDtypeStruct
    dma = pltpu.SemaphoreType.DMA
    feat = features.reshape(2, EDGE, EDGE)
    n_groups = tiles.shape[0] // GROUP

    feat_parts = ring(jnp.concatenate(along_y(feat), axis=0), ALONG_Z)
    n_feat = len(feat_parts)
    degs = [
        call(
            functools.partial(degree_kernel, i * GROUP),
            shape((16, 8, EDGE), F32),
            [SMEM, VMEM],
            mib=4,
            flops=2**32,
            bytes_accessed=2**20,
        )(slots, tiles)
        for i in range(n_groups)
    ]
    block = shape((1056, EDGE), F32)
    keep, send = call(
        functools.partial(first_kernel, n_feat),
        (block, block),
        [SMEM] * 2 + [VMEM] * 5 + [ANY] * n_feat,
        [
            pltpu.VMEM((64, EDGE, EDGE), BF16),
            pltpu.VMEM((2112, EDGE), F32),
            dma((n_feat,)),
        ],
        mib=8,
        flops=2**29,
        bytes_accessed=2**23,
    )(offs, cols, tiles, *degs, *feat_parts)
    sums = call(join_first_kernel, (shape((264, EDGE), F32),) * 4, [VMEM] * 2)(
        keep, to_sibling(send)
    )
    agg, inv = call(
        aggregate_kernel, (shape((2, EDGE, EDGE), BF16), shape((2, EDGE), F32)), [VMEM] * 4
    )(sums[0], along_x(sums[1], 1), along_x(sums[2], 2), along_x(sums[3], 3))
    agg_parts = ring(jnp.concatenate(along_y(agg), axis=0), ALONG_Z)
    weights = jnp.concatenate([self_first, neigh_first], axis=0)
    bias = bias_first.reshape(1, -1)

    lacking = ((0, 256 - classes), (0, 0))
    self_t = jnp.pad(self_second.T, lacking)
    neigh_t = jnp.pad(neigh_second.T, lacking)
    bias_wide = jnp.broadcast_to(jnp.pad(bias_second, (0, PAD - classes))[:, None], (PAD, EDGE))
    half = shape((8, PAD, EDGE), BF16)
    agg_second, keep, send, mine, hid = call(
        functools.partial(second_kernel, n_feat),
        (
            shape((16, hid_size, EDGE), BF16),
            half,
            half,
            shape((2, hid_size, EDGE), BF16),
            shape((64, hid_size, EDGE), BF16),
        ),
        [SMEM] * 2 + [VMEM] * (4 + 2 * n_feat),
        [pltpu.VMEM((16, hid_size, EDGE), F32)],
        mib=14,
        flops=2**31,
        bytes_accessed=2**23,
    )(slots, cols, tiles, neigh_t, weights, bias, *feat_parts, *agg_parts)
    sums = call(join_second_kernel, (shape((2, PAD, EDGE), BF16),) * 4, [VMEM] * 2)(
        keep, to_sibling(send)
    )
    lg, w, grad_self, grad_bias = call(
        functools.partial(loss_kernel, classes, scale),
        (
            shape((2, PAD, EDGE), BF16),
            shape((2, PAD, EDGE), BF16),
            shape((PAD, hid_size), F32),
            shape((8, PAD), F32),
        ),
        [VMEM] * 10,
    )(
        sums[0],
        along_x(sums[1], 1),
        along_x(sums[2], 2),
        along_x(sums[3], 3),
        mine,
        self_t,
        bias_wide,
        labels.reshape(2, EDGE),
        train_mask.reshape(2, EDGE),
        inv,
    )
    w_parts = [w, along_x(w, 1), along_x(w, 3), along_x(w, 2)]
    w_parts.append(to_sibling(jnp.concatenate(w_parts, axis=0)))
    grads = call(
        functools.partial(last_kernel, n_feat),
        shape((1280, EDGE), BF16),
        [SMEM] * 2 + [VMEM] * 13 + [ANY] * (2 * n_feat),
        [
            pltpu.VMEM((64, EDGE, 2 * EDGE), BF16),
            pltpu.VMEM((64, hid_size, EDGE), F32),
            pltpu.VMEM((16, hid_size, EDGE), BF16),
            dma((2 * n_feat,)),
        ],
        mib=22,
        flops=2**31,
        bytes_accessed=2**24,
    )(
        slots, cols, *w_parts, hid, tiles, agg_second, lg, self_t, neigh_t, grad_self,
        grad_bias, *feat_parts, *agg_parts
    )
    out = call(
        functools.partial(unpack_kernel, classes),
        (
            shape(self_first.shape, F32),
            shape(neigh_first.shape, F32),
            shape((1, hid_size), F32),
            shape((classes, hid_size), F32),
            shape((classes, hid_size), F32),
            shape((1, 256), F32),
        ),
        [VMEM],
    )(sum_everywhere(grads))
    return (
        out[0],
        out[1],
        out[2].reshape(hid_size),
        out[3].T,
        out[4].T,
        out[5].reshape(256)[:classes],
    )


def solution(mesh):
    in_specs = (
        P(("row", "col"), None),
        P("row", "col", None, None, None),
        P("row", "col", None),
        P("row", "col", None),
        P(("row", "col")),
        P(("row", "col")),
        P(),
        P(),
        P(),
        P(),
        P(),
        P(),
    )
    out_specs = (P(), P(), P(), P(), P(), P())
    return jax.shard_map(
        on_device, mesh=mesh, in_specs=in_specs, out_specs=out_specs, check_vma=False
    )
```

profile of v0, /device:TPU:1, one launch (start us, length us, event | category | flops | bytes accessed | tf_op | source)
XLA Modules:
  0.0 178.2 jit_solution(172667404356903035)
XLA Ops:
  0.6 3.8 %collective-permute-start.2 = (bf16[2,128,128]{2,1,0:T(8,128)(2,1)}, bf16[2,128,128]{2,1,0:T(8,128)(2,1)S(1)}, u32[]{:S(2)}, u32[]{:S(2)}) collective-permute-start(bf16[2,128,128]{2,1,0:T(8,128)(2,1)} %bitcast.55), channel_id=1, source_target_pairs={{0,128},{64,192},{128,0},{192,64},{8,136},{72,200},{136,8},{200,72... | collective-permute-start | bytes 196616 | tf_op jit(solution)/shard_map/ppermute | solution.py:46
  10.8 5.5 %collective-permute-start.4 = (bf16[8,128,128]{2,1,0:T(8,128)(2,1)S(1)}, bf16[8,128,128]{2,1,0:T(8,128)(2,1)S(1)}, u32[]{:S(2)}, u32[]{:S(2)}) collective-permute-start(bf16[8,128,128]{2,1,0:T(8,128)(2,1)S(1)} %pad_maximum_fusion.1.refs_0_), channel_id=1, source_target_pairs={{0,56},{8,0},{16,8},{24,16},{32,24},{40,32},{48,40},{56,48},{64,12... | collective-permute-start | bytes 786440 | tf_op jit(solution)/shard_map/ppermute | solution.py:46
  18.5 2.6 %shard_map.166.d3 = f32[16,8,128]{2,1,0:T(8,128)S(1)} custom-call(s32[128]{0:T(128)S(1)} %get-tuple-element.61.slots, bf16[128,128,128]{2,1,0:T(8,128)(2,1)S(1)} %bitcast.41), custom_call_target="tpu_custom_call" | custom-call | flops 4294967296 | bytes 1048576 | tf_op jit(solution)/shard_map/pallas_call | solution.py:394
  21.1 2.8 %collective-permute-start.6 = (bf16[8,128,128]{2,1,0:T(8,128)(2,1)S(1)}, bf16[8,128,128]{2,1,0:T(8,128)(2,1)S(1)}, u32[]{:S(2)}, u32[]{:S(2)}) collective-permute-start(bf16[8,128,128]{2,1,0:T(8,128)(2,1)S(1)} %collective-permute-done.4.refs_2_), channel_id=1, source_target_pairs={{0,56},{8,0},{16,8},{24,16},{32,24},{40,32},{48,40},{56,48},{64,12... | collective-permute-start | bytes 786440 | tf_op jit(solution)/shard_map/ppermute | solution.py:46
  23.9 2.6 %shard_map.165.d2 = f32[16,8,128]{2,1,0:T(8,128)S(1)} custom-call(s32[128]{0:T(128)S(1)} %get-tuple-element.61.slots, bf16[128,128,128]{2,1,0:T(8,128)(2,1)S(1)} %bitcast.42), custom_call_target="tpu_custom_call" | custom-call | flops 4294967296 | bytes 1048576 | tf_op jit(solution)/shard_map/pallas_call | solution.py:394
  27.2 3.1 %collective-permute-start.8 = (bf16[8,128,128]{2,1,0:T(8,128)(2,1)S(1)}, bf16[8,128,128]{2,1,0:T(8,128)(2,1)S(1)}, u32[]{:S(2)}, u32[]{:S(2)}) collective-permute-start(bf16[8,128,128]{2,1,0:T(8,128)(2,1)S(1)} %collective-permute-done.6.refs_4_), channel_id=1, source_target_pairs={{0,56},{8,0},{16,8},{24,16},{32,24},{40,32},{48,40},{56,48},{64,12... | collective-permute-start | bytes 786440 | tf_op jit(solution)/shard_map/ppermute | solution.py:46
  30.3 2.6 %shard_map.164.d1 = f32[16,8,128]{2,1,0:T(8,128)S(1)} custom-call(s32[128]{0:T(128)S(1)} %get-tuple-element.61.slots, bf16[128,128,128]{2,1,0:T(8,128)(2,1)S(1)} %bitcast.43), custom_call_target="tpu_custom_call" | custom-call | flops 4294967296 | bytes 1048576 | tf_op jit(solution)/shard_map/pallas_call | solution.py:394
  33.6 3.2 %collective-permute-start.10 = (bf16[4,128,128]{2,1,0:T(8,128)(2,1)S(1)}, bf16[4,128,128]{2,1,0:T(8,128)(2,1)S(1)}, u32[]{:S(2)}, u32[]{:S(2)}) collective-permute-start(bf16[4,128,128]{2,1,0:T(8,128)(2,1)S(1)} %slice.25), channel_id=1, source_target_pairs={{0,56},{8,0},{16,8},{24,16},{32,24},{40,32},{48,40},{56,48},{64,12... | collective-permute-start | bytes 393224 | tf_op jit(solution)/shard_map/ppermute | solution.py:46
  36.9 2.6 %shard_map.163.d0 = f32[16,8,128]{2,1,0:T(8,128)S(1)} custom-call(s32[128]{0:T(128)S(1)} %get-tuple-element.61.slots, bf16[128,128,128]{2,1,0:T(8,128)(2,1)S(1)} %bitcast.44), custom_call_target="tpu_custom_call" | custom-call | flops 4294967296 | bytes 1048576 | tf_op jit(solution)/shard_map/pallas_call | solution.py:394
  39.6 3.4 %collective-permute-done.9.refs_7_ = bf16[4,128,128]{2,1,0:T(8,128)(2,1)S(1)} collective-permute-done((bf16[4,128,128]{2,1,0:T(8,128)(2,1)S(1)}, bf16[4,128,128]{2,1,0:T(8,128)(2,1)S(1)}, u32[]{:S(2)}, u32[]{:S(2)}) %collective-permute-start.9) | collective-permute-done | bytes 131104 | tf_op jit(solution)/shard_map/ppermute | solution.py:46
  43.0 3.3 %shard_map.167 = (f32[1056,128]{1,0:T(8,128)S(1)}, f32[1056,128]{1,0:T(8,128)S(1)}) custom-call(s32[128]{0:T(128)S(1)} %get-tuple-element.60.offs, s32[128]{0:T(128)S(1)} %get-tuple-element.62.cols, bf16[128,128,128]{2,1,0:T(8,128)(2,1)S(1)} %bitcast.45, f32[16,8,128]{2,1,0:T(8,128)S(1)} %shard_map.163.d0, f32[16,8,128]{2,1,0:T(8,128)S(1)} %shard_map.164.d1, ...), custom_call_target="tpu_custom_call" | custom-call | flops 536870912 | bytes 8388608 | tf_op jit(solution)/shard_map/pallas_call | solution.py:405
  46.2 6.6 %collective-permute-start.11 = (f32[1056,128]{1,0:T(8,128)S(1)}, f32[1056,128]{1,0:T(8,128)S(1)}, u32[]{:S(2)}, u32[]{:S(2)}) collective-permute-start(f32[1056,128]{1,0:T(8,128)S(1)} %get-tuple-element.34), channel_id=1, source_target_pairs={{0,1},{1,0},{2,3},{3,2},{4,5},{5,4},{6,7},{7,6},{8,9},{9,8},{10,11... | collective-permute-start | bytes 1622024 | tf_op jit(solution)/shard_map/ppermute | solution.py:85
  55.7 2.4 %collective-permute-start.13 = (f32[264,128]{1,0:T(8,128)S(1)}, f32[264,128]{1,0:T(8,128)S(1)}, u32[]{:S(2)}, u32[]{:S(2)}) collective-permute-start(f32[264,128]{1,0:T(8,128)S(1)} %get-tuple-element.37), channel_id=1, source_target_pairs={{0,4},{1,5},{2,6},{3,7},{4,0},{5,1},{6,2},{7,3},{8,12},{9,13},{10,... | collective-permute-start | bytes 405512 | tf_op jit(solution)/shard_map/ppermute | solution.py:89
  60.5 3.9 %collective-permute-done.13.s2 = f32[264,128]{1,0:T(8,128)S(1)} collective-permute-done((f32[264,128]{1,0:T(8,128)S(1)}, f32[264,128]{1,0:T(8,128)S(1)}, u32[]{:S(2)}, u32[]{:S(2)}) %collective-permute-start.13) | collective-permute-done | bytes 135200 | tf_op jit(solution)/shard_map/ppermute | solution.py:89
  66.2 4.7 %collective-permute-done.15 = bf16[2,128,128]{2,1,0:T(8,128)(2,1)S(1)} collective-permute-done((bf16[2,128,128]{2,1,0:T(8,128)(2,1)S(1)}, bf16[2,128,128]{2,1,0:T(8,128)(2,1)S(1)}, u32[]{:S(2)}, u32[]{:S(2)}) %collective-permute-start.15) | collective-permute-done | bytes 65568 | tf_op jit(solution)/shard_map/ppermute | solution.py:46
  72.5 3.8 %collective-permute-done.19.refs_11_ = bf16[8,128,128]{2,1,0:T(8,128)(2,1)S(1)} collective-permute-done((bf16[8,128,128]{2,1,0:T(8,128)(2,1)S(1)}, bf16[8,128,128]{2,1,0:T(8,128)(2,1)S(1)}, u32[]{:S(2)}, u32[]{:S(2)}) %collective-permute-start.19) | collective-permute-done | bytes 262176 | tf_op jit(solution)/shard_map/ppermute | solution.py:46
  78.0 4.0 %collective-permute-done.21.refs_13_ = bf16[8,128,128]{2,1,0:T(8,128)(2,1)S(1)} collective-permute-done((bf16[8,128,128]{2,1,0:T(8,128)(2,1)S(1)}, bf16[8,128,128]{2,1,0:T(8,128)(2,1)S(1)}, u32[]{:S(2)}, u32[]{:S(2)}) %collective-permute-start.21) | collective-permute-done | bytes 262176 | tf_op jit(solution)/shard_map/ppermute | solution.py:46
  82.0 2.4 %collective-permute-start.23 = (bf16[8,128,128]{2,1,0:T(8,128)(2,1)S(1)}, bf16[8,128,128]{2,1,0:T(8,128)(2,1)S(1)}, u32[]{:S(2)}, u32[]{:S(2)}) collective-permute-start(bf16[8,128,128]{2,1,0:T(8,128)(2,1)S(1)} %collective-permute-done.21.refs_13_), channel_id=1, source_target_pairs={{0,56},{8,0},{16,8},{24,16},{32,24},{40,32},{48,40},{56,48},{64,12... | collective-permute-start | bytes 786440 | tf_op jit(solution)/shard_map/ppermute | solution.py:46
  84.3 4.4 %collective-permute-done.23.refs_15_ = bf16[8,128,128]{2,1,0:T(8,128)(2,1)S(1)} collective-permute-done((bf16[8,128,128]{2,1,0:T(8,128)(2,1)S(1)}, bf16[8,128,128]{2,1,0:T(8,128)(2,1)S(1)}, u32[]{:S(2)}, u32[]{:S(2)}) %collective-permute-start.23) | collective-permute-done | bytes 262176 | tf_op jit(solution)/shard_map/ppermute | solution.py:46
  91.1 3.2 %collective-permute-done.25.refs_17_ = bf16[4,128,128]{2,1,0:T(8,128)(2,1)S(1)} collective-permute-done((bf16[4,128,128]{2,1,0:T(8,128)(2,1)S(1)}, bf16[4,128,128]{2,1,0:T(8,128)(2,1)S(1)}, u32[]{:S(2)}, u32[]{:S(2)}) %collective-permute-start.25) | collective-permute-done | bytes 131104 | tf_op jit(solution)/shard_map/ppermute | solution.py:46
  94.3 2.9 %collective-permute-done.24.refs_16_ = bf16[4,128,128]{2,1,0:T(8,128)(2,1)S(1)} collective-permute-done((bf16[4,128,128]{2,1,0:T(8,128)(2,1)S(1)}, bf16[4,128,128]{2,1,0:T(8,128)(2,1)S(1)}, u32[]{:S(2)}, u32[]{:S(2)}) %collective-permute-start.24) | collective-permute-done | bytes 131104 | tf_op jit(solution)/shard_map/ppermute | solution.py:46
  97.3 6.9 %shard_map.170 = (bf16[16,256,128]{2,1,0:T(8,128)(2,1)S(1)}, bf16[8,176,128]{2,1,0:T(8,128)(2,1)S(1)}, bf16[8,176,128]{2,1,0:T(8,128)(2,1)S(1)}, bf16[2,256,128]...) custom-call(s32[128]{0:T(128)S(1)} %get-tuple-element.61.slots, s32[128]{0:T(128)S(1)} %get-tuple-element.62.cols, ...), custom_call_target="tpu_custom_call" | custom-call | flops 2147483648 | bytes 8388608 | tf_op jit(solution)/shard_map/pallas_call | solution.py:433
  104.2 6.7 %collective-permute-start.26 = (bf16[8,176,128]{2,1,0:T(8,128)(2,1)S(1)}, bf16[8,176,128]{2,1,0:T(8,128)(2,1)S(1)}, u32[]{:S(2)}, u32[]{:S(2)}) collective-permute-start(bf16[8,176,128]{2,1,0:T(8,128)(2,1)S(1)} %get-tuple-element.41), channel_id=1, source_target_pairs={{0,1},{1,0},{2,3},{3,2},{4,5},{5,4},{6,7},{7,6},{8,9},{9,8},{10,11... | collective-permute-start | bytes 1081352 | tf_op jit(solution)/shard_map/ppermute | solution.py:85
  113.5 2.8 %collective-permute-start.28 = (bf16[2,176,128]{2,1,0:T(8,128)(2,1)S(1)}, bf16[2,176,128]{2,1,0:T(8,128)(2,1)S(1)}, u32[]{:S(2)}, u32[]{:S(2)}) collective-permute-start(bf16[2,176,128]{2,1,0:T(8,128)(2,1)S(1)} %get-tuple-element.44), channel_id=1, source_target_pairs={{0,4},{1,5},{2,6},{3,7},{4,0},{5,1},{6,2},{7,3},{8,12},{9,13},{10,... | collective-permute-start | bytes 270344 | tf_op jit(solution)/shard_map/ppermute | solution.py:89
  118.1 2.5 %collective-permute-done.28.s2 = bf16[2,176,128]{2,1,0:T(8,128)(2,1)S(1)} collective-permute-done((bf16[2,176,128]{2,1,0:T(8,128)(2,1)S(1)}, bf16[2,176,128]{2,1,0:T(8,128)(2,1)S(1)}, u32[]{:S(2)}, u32[]{:S(2)}) %collective-permute-start.28) | collective-permute-done | bytes 90144 | tf_op jit(solution)/shard_map/ppermute | solution.py:89
  121.4 2.4 %collective-permute-start.32 = (bf16[2,176,128]{2,1,0:T(8,128)(2,1)S(1)}, bf16[2,176,128]{2,1,0:T(8,128)(2,1)S(1)}, u32[]{:S(2)}, u32[]{:S(2)}) collective-permute-start(bf16[2,176,128]{2,1,0:T(8,128)(2,1)S(1)} %get-tuple-element.48.w0), channel_id=1, source_target_pairs={{0,4},{1,5},{2,6},{3,7},{4,0},{5,1},{6,2},{7,3},{8,12},{9,13},{10,... | collective-permute-start | bytes 270344 | tf_op jit(solution)/shard_map/ppermute | solution.py:89
  129.1 3.8 %collective-permute-start.33 = (bf16[8,176,128]{2,1,0:T(8,128)(2,1)S(1)}, bf16[8,176,128]{2,1,0:T(8,128)(2,1)S(1)}, u32[]{:S(2)}, u32[]{:S(2)}) collective-permute-start(bf16[8,176,128]{2,1,0:T(8,128)(2,1)S(1)} %pad_maximum_fusion), channel_id=1, source_target_pairs={{0,1},{1,0},{2,3},{3,2},{4,5},{5,4},{6,7},{7,6},{8,9},{9,8},{10,11... | collective-permute-start | bytes 1081352 | tf_op jit(solution)/shard_map/ppermute | solution.py:85
  134.2 9.4 %shard_map.173 = bf16[1280,128]{1,0:T(8,128)(2,1)S(1)} custom-call(s32[128]{0:T(128)S(1)} %get-tuple-element.61.slots, s32[128]{0:T(128)S(1)} %get-tuple-element.62.cols, bf16[2,176,128]{2,1,0:T(8,128)(2,1)S(1)} %get-tuple-element.48.w0, bf16[2,176,128]{2,1,0:T(8,128)(2,1)S(1)} %collective-permute-done.30.w1, ...), custom_call_target="tpu_custom_call" | custom-call | flops 2147483648 | bytes 16777216 | tf_op jit(solution)/shard_map/pallas_call | solution.py:474
  143.6 11.6 %all_to_all.10.x = bf16[16,80,128]{2,1,0:T(8,128)(2,1)S(1)} all-to-all(bf16[16,80,128]{2,1,0:T(8,128)(2,1)S(1)} %bitcast.49), channel_id=1, replica_groups={{0,2,4,6,64,66,68,70,128,130,132,134,192,194,196,198},{1,3,5,7,65,67,69..., dimensions={0} | all-to-all | bytes 655360 | tf_op jit(solution)/shard_map/all_to_all | solution.py:353
  155.3 2.7 %collective-permute-start.35 = (bf16[80,128]{1,0:T(8,128)(2,1)S(1)}, bf16[80,128]{1,0:T(8,128)(2,1)S(1)}, u32[]{:S(2)}, u32[]{:S(2)}) collective-permute-start(bf16[80,128]{1,0:T(8,128)(2,1)S(1)} %shard_map.174.a), channel_id=1, source_target_pairs={{0,8},{1,9},{2,10},{3,11},{4,12},{5,13},{6,14},{7,15},{8,0},{9,1},... | collective-permute-start | bytes 61448 | tf_op jit(solution)/shard_map/ppermute | solution.py:355
  161.2 4.0 %collective-permute-start.37 = (bf16[80,128]{1,0:T(8,128)(2,1)S(1)}, bf16[80,128]{1,0:T(8,128)(2,1)S(1)}, u32[]{:S(2)}, u32[]{:S(2)}) collective-permute-start(bf16[80,128]{1,0:T(8,128)(2,1)S(1)} %shard_map.175.a), channel_id=1, source_target_pairs={{0,16},{8,24},{16,0},{24,8},{32,48},{40,56},{48,32},{56,40},{64,80... | collective-permute-start | bytes 61448 | tf_op jit(solution)/shard_map/ppermute | solution.py:357
  166.8 10.5 %all_to_all.11 = bf16[16,80,128]{2,1,0:T(8,128)(2,1)S(1)} all-to-all(bf16[16,80,128]{2,1,0:T(8,128)(2,1)S(1)} %shard_map.176), channel_id=1, replica_groups={{0,2,4,6,64,66,68,70,128,130,132,134,192,194,196,198},{1,3,5,7,65,67,69..., dimensions={0} | all-to-all | bytes 655360 | tf_op jit(solution)/shard_map/all_to_all | solution.py:359
  (101 shorter events, 40.2 us)
Async XLA Ops:
  0.6 6.0 %collective-permute-start.2 = (bf16[2,128,128]{2,1,0:T(8,128)(2,1)}, bf16[2,128,128]{2,1,0:T(8,128)(2,1)S(1)}, u32[]{:S(2)}, u32[]{:S(2)}) collective-permute-start(bf16[2,128,128]{2,1,0:T(8,128)(2,1)} %bitcast.55), channel_id=1, source_target_pairs={{0,128},{64,192},{128,0},{192,64},{8,136},{72,200},{136,8},{200,72... | collective-permute-start | bytes 196616 | tf_op jit(solution)/shard_map/ppermute | solution.py:46
  10.8 10.3 %collective-permute-start.4 = (bf16[8,128,128]{2,1,0:T(8,128)(2,1)S(1)}, bf16[8,128,128]{2,1,0:T(8,128)(2,1)S(1)}, u32[]{:S(2)}, u32[]{:S(2)}) collective-permute-start(bf16[8,128,128]{2,1,0:T(8,128)(2,1)S(1)} %pad_maximum_fusion.1.refs_0_), channel_id=1, source_target_pairs={{0,56},{8,0},{16,8},{24,16},{32,24},{40,32},{48,40},{56,48},{64,12... | collective-permute-start | bytes 786440 | tf_op jit(solution)/shard_map/ppermute | solution.py:46
  16.3 7.5 %collective-permute-start.3 = (bf16[8,128,128]{2,1,0:T(8,128)(2,1)S(1)}, bf16[8,128,128]{2,1,0:T(8,128)(2,1)S(1)}, u32[]{:S(2)}, u32[]{:S(2)}) collective-permute-start(bf16[8,128,128]{2,1,0:T(8,128)(2,1)S(1)} %pad_maximum_fusion.1.refs_0_), channel_id=1, source_target_pairs={{0,8},{8,16},{16,24},{24,32},{32,40},{40,48},{48,56},{56,0},{64,72... | collective-permute-start | bytes 786440 | tf_op jit(solution)/shard_map/ppermute | solution.py:46
  21.1 6.1 %collective-permute-start.6 = (bf16[8,128,128]{2,1,0:T(8,128)(2,1)S(1)}, bf16[8,128,128]{2,1,0:T(8,128)(2,1)S(1)}, u32[]{:S(2)}, u32[]{:S(2)}) collective-permute-start(bf16[8,128,128]{2,1,0:T(8,128)(2,1)S(1)} %collective-permute-done.4.refs_2_), channel_id=1, source_target_pairs={{0,56},{8,0},{16,8},{24,16},{32,24},{40,32},{48,40},{56,48},{64,12... | collective-permute-start | bytes 786440 | tf_op jit(solution)/shard_map/ppermute | solution.py:46
  23.8 6.4 %collective-permute-start.5 = (bf16[8,128,128]{2,1,0:T(8,128)(2,1)S(1)}, bf16[8,128,128]{2,1,0:T(8,128)(2,1)S(1)}, u32[]{:S(2)}, u32[]{:S(2)}) collective-permute-start(bf16[8,128,128]{2,1,0:T(8,128)(2,1)S(1)} %collective-permute-done.3.refs_1_), channel_id=1, source_target_pairs={{0,8},{8,16},{16,24},{24,32},{32,40},{40,48},{48,56},{56,0},{64,72... | collective-permute-start | bytes 786440 | tf_op jit(solution)/shard_map/ppermute | solution.py:46
  27.2 6.4 %collective-permute-start.8 = (bf16[8,128,128]{2,1,0:T(8,128)(2,1)S(1)}, bf16[8,128,128]{2,1,0:T(8,128)(2,1)S(1)}, u32[]{:S(2)}, u32[]{:S(2)}) collective-permute-start(bf16[8,128,128]{2,1,0:T(8,128)(2,1)S(1)} %collective-permute-done.6.refs_4_), channel_id=1, source_target_pairs={{0,56},{8,0},{16,8},{24,16},{32,24},{40,32},{48,40},{56,48},{64,12... | collective-permute-start | bytes 786440 | tf_op jit(solution)/shard_map/ppermute | solution.py:46
  30.3 6.5 %collective-permute-start.7 = (bf16[8,128,128]{2,1,0:T(8,128)(2,1)S(1)}, bf16[8,128,128]{2,1,0:T(8,128)(2,1)S(1)}, u32[]{:S(2)}, u32[]{:S(2)}) collective-permute-start(bf16[8,128,128]{2,1,0:T(8,128)(2,1)S(1)} %collective-permute-done.5.refs_3_), channel_id=1, source_target_pairs={{0,8},{8,16},{16,24},{24,32},{32,40},{40,48},{48,56},{56,0},{64,72... | collective-permute-start | bytes 786440 | tf_op jit(solution)/shard_map/ppermute | solution.py:46
  33.6 5.9 %collective-permute-start.10 = (bf16[4,128,128]{2,1,0:T(8,128)(2,1)S(1)}, bf16[4,128,128]{2,1,0:T(8,128)(2,1)S(1)}, u32[]{:S(2)}, u32[]{:S(2)}) collective-permute-start(bf16[4,128,128]{2,1,0:T(8,128)(2,1)S(1)} %slice.25), channel_id=1, source_target_pairs={{0,56},{8,0},{16,8},{24,16},{32,24},{40,32},{48,40},{56,48},{64,12... | collective-permute-start | bytes 393224 | tf_op jit(solution)/shard_map/ppermute | solution.py:46
  36.8 6.1 %collective-permute-start.9 = (bf16[4,128,128]{2,1,0:T(8,128)(2,1)S(1)}, bf16[4,128,128]{2,1,0:T(8,128)(2,1)S(1)}, u32[]{:S(2)}, u32[]{:S(2)}) collective-permute-start(bf16[4,128,128]{2,1,0:T(8,128)(2,1)S(1)} %slice.24), channel_id=1, source_target_pairs={{0,8},{8,16},{16,24},{24,32},{32,40},{40,48},{48,56},{56,0},{64,72... | collective-permute-start | bytes 393224 | tf_op jit(solution)/shard_map/ppermute | solution.py:46
  46.2 8.1 %collective-permute-start.11 = (f32[1056,128]{1,0:T(8,128)S(1)}, f32[1056,128]{1,0:T(8,128)S(1)}, u32[]{:S(2)}, u32[]{:S(2)}) collective-permute-start(f32[1056,128]{1,0:T(8,128)S(1)} %get-tuple-element.34), channel_id=1, source_target_pairs={{0,1},{1,0},{2,3},{3,2},{4,5},{5,4},{6,7},{7,6},{8,9},{9,8},{10,11... | collective-permute-start | bytes 1622024 | tf_op jit(solution)/shard_map/ppermute | solution.py:85
  54.4 6.1 %collective-permute-start.12 = (f32[264,128]{1,0:T(8,128)S(1)}, f32[264,128]{1,0:T(8,128)S(1)}, u32[]{:S(2)}, u32[]{:S(2)}) collective-permute-start(f32[264,128]{1,0:T(8,128)S(1)} %get-tuple-element.36), channel_id=1, source_target_pairs={{0,2},{1,3},{2,4},{3,5},{4,6},{5,7},{6,0},{7,1},{8,10},{9,11},{10,... | collective-permute-start | bytes 405512 | tf_op jit(solution)/shard_map/ppermute | solution.py:89
  55.7 8.7 %collective-permute-start.13 = (f32[264,128]{1,0:T(8,128)S(1)}, f32[264,128]{1,0:T(8,128)S(1)}, u32[]{:S(2)}, u32[]{:S(2)}) collective-permute-start(f32[264,128]{1,0:T(8,128)S(1)} %get-tuple-element.37), channel_id=1, source_target_pairs={{0,4},{1,5},{2,6},{3,7},{4,0},{5,1},{6,2},{7,3},{8,12},{9,13},{10,... | collective-permute-start | bytes 405512 | tf_op jit(solution)/shard_map/ppermute | solution.py:89
  58.2 6.2 %collective-permute-start.14 = (f32[264,128]{1,0:T(8,128)S(1)}, f32[264,128]{1,0:T(8,128)S(1)}, u32[]{:S(2)}, u32[]{:S(2)}) collective-permute-start(f32[264,128]{1,0:T(8,128)S(1)} %get-tuple-element.38), channel_id=1, source_target_pairs={{0,6},{1,7},{2,0},{3,1},{4,2},{5,3},{6,4},{7,5},{8,14},{9,15},{10,... | collective-permute-start | bytes 405512 | tf_op jit(solution)/shard_map/ppermute | solution.py:89
  64.5 6.4 %collective-permute-start.17 = (bf16[2,128,128]{2,1,0:T(8,128)(2,1)S(1)}, bf16[2,128,128]{2,1,0:T(8,128)(2,1)S(1)}, u32[]{:S(2)}, u32[]{:S(2)}) collective-permute-start(bf16[2,128,128]{2,1,0:T(8,128)(2,1)S(1)} %get-tuple-element.39), channel_id=1, source_target_pairs={{0,128},{64,192},{128,0},{192,64},{8,136},{72,200},{136,8},{200,72... | collective-permute-start | bytes 196616 | tf_op jit(solution)/shard_map/ppermute | solution.py:46
  64.6 6.3 %collective-permute-start.16 = (bf16[2,128,128]{2,1,0:T(8,128)(2,1)S(1)}, bf16[2,128,128]{2,1,0:T(8,128)(2,1)S(1)}, u32[]{:S(2)}, u32[]{:S(2)}) collective-permute-start(bf16[2,128,128]{2,1,0:T(8,128)(2,1)S(1)} %get-tuple-element.39), channel_id=1, source_target_pairs={{0,192},{64,0},{128,64},{192,128},{8,200},{72,8},{136,72},{200,136... | collective-permute-start | bytes 196616 | tf_op jit(solution)/shard_map/ppermute | solution.py:46
  71.0 5.3 %collective-permute-start.19 = (bf16[8,128,128]{2,1,0:T(8,128)(2,1)S(1)}, bf16[8,128,128]{2,1,0:T(8,128)(2,1)S(1)}, u32[]{:S(2)}, u32[]{:S(2)}) collective-permute-start(bf16[8,128,128]{2,1,0:T(8,128)(2,1)S(1)} %constant_dynamic-update-slice_fusion.refs_9_), channel_id=1, source_target_pairs={{0,56},{8,0},{16,8},{24,16},{32,24},{40,32},{48,40},{56,48},{64,12... | collective-permute-start | bytes 786440 | tf_op jit(solution)/shard_map/ppermute | solution.py:46
  71.1 6.9 %collective-permute-start.18 = (bf16[8,128,128]{2,1,0:T(8,128)(2,1)S(1)}, bf16[8,128,128]{2,1,0:T(8,128)(2,1)S(1)}, u32[]{:S(2)}, u32[]{:S(2)}) collective-permute-start(bf16[8,128,128]{2,1,0:T(8,128)(2,1)S(1)} %constant_dynamic-update-slice_fusion.refs_9_), channel_id=1, source_target_pairs={{0,8},{8,16},{16,24},{24,32},{32,40},{40,48},{48,56},{56,0},{64,72... | collective-permute-start | bytes 786440 | tf_op jit(solution)/shard_map/ppermute | solution.py:46
  76.3 5.7 %collective-permute-start.21 = (bf16[8,128,128]{2,1,0:T(8,128)(2,1)S(1)}, bf16[8,128,128]{2,1,0:T(8,128)(2,1)S(1)}, u32[]{:S(2)}, u32[]{:S(2)}) collective-permute-start(bf16[8,128,128]{2,1,0:T(8,128)(2,1)S(1)} %collective-permute-done.19.refs_11_), channel_id=1, source_target_pairs={{0,56},{8,0},{16,8},{24,16},{32,24},{40,32},{48,40},{56,48},{64,12... | collective-permute-start | bytes 786440 | tf_op jit(solution)/shard_map/ppermute | solution.py:46
  77.9 6.4 %collective-permute-start.20 = (bf16[8,128,128]{2,1,0:T(8,128)(2,1)S(1)}, bf16[8,128,128]{2,1,0:T(8,128)(2,1)S(1)}, u32[]{:S(2)}, u32[]{:S(2)}) collective-permute-start(bf16[8,128,128]{2,1,0:T(8,128)(2,1)S(1)} %collective-permute-done.18.refs_10_), channel_id=1, source_target_pairs={{0,8},{8,16},{16,24},{24,32},{32,40},{40,48},{48,56},{56,0},{64,72... | collective-permute-start | bytes 786440 | tf_op jit(solution)/shard_map/ppermute | solution.py:46
  82.0 6.8 %collective-permute-start.23 = (bf16[8,128,128]{2,1,0:T(8,128)(2,1)S(1)}, bf16[8,128,128]{2,1,0:T(8,128)(2,1)S(1)}, u32[]{:S(2)}, u32[]{:S(2)}) collective-permute-start(bf16[8,128,128]{2,1,0:T(8,128)(2,1)S(1)} %collective-permute-done.21.refs_13_), channel_id=1, source_target_pairs={{0,56},{8,0},{16,8},{24,16},{32,24},{40,32},{48,40},{56,48},{64,12... | collective-permute-start | bytes 786440 | tf_op jit(solution)/shard_map/ppermute | solution.py:46
  84.3 6.6 %collective-permute-start.22 = (bf16[8,128,128]{2,1,0:T(8,128)(2,1)S(1)}, bf16[8,128,128]{2,1,0:T(8,128)(2,1)S(1)}, u32[]{:S(2)}, u32[]{:S(2)}) collective-permute-start(bf16[8,128,128]{2,1,0:T(8,128)(2,1)S(1)} %collective-permute-done.20.refs_12_), channel_id=1, source_target_pairs={{0,8},{8,16},{16,24},{24,32},{32,40},{40,48},{48,56},{56,0},{64,72... | collective-permute-start | bytes 786440 | tf_op jit(solution)/shard_map/ppermute | solution.py:46
  88.8 5.6 %collective-permute-start.25 = (bf16[4,128,128]{2,1,0:T(8,128)(2,1)S(1)}, bf16[4,128,128]{2,1,0:T(8,128)(2,1)S(1)}, u32[]{:S(2)}, u32[]{:S(2)}) collective-permute-start(bf16[4,128,128]{2,1,0:T(8,128)(2,1)S(1)} %slice.27), channel_id=1, source_target_pairs={{0,56},{8,0},{16,8},{24,16},{32,24},{40,32},{48,40},{56,48},{64,12... | collective-permute-start | bytes 393224 | tf_op jit(solution)/shard_map/ppermute | solution.py:46
  91.0 6.3 %collective-permute-start.24 = (bf16[4,128,128]{2,1,0:T(8,128)(2,1)S(1)}, bf16[4,128,128]{2,1,0:T(8,128)(2,1)S(1)}, u32[]{:S(2)}, u32[]{:S(2)}) collective-permute-start(bf16[4,128,128]{2,1,0:T(8,128)(2,1)S(1)} %slice.26), channel_id=1, source_target_pairs={{0,8},{8,16},{16,24},{24,32},{32,40},{40,48},{48,56},{56,0},{64,72... | collective-permute-start | bytes 393224 | tf_op jit(solution)/shard_map/ppermute | solution.py:46
  104.2 8.1 %collective-permute-start.26 = (bf16[8,176,128]{2,1,0:T(8,128)(2,1)S(1)}, bf16[8,176,128]{2,1,0:T(8,128)(2,1)S(1)}, u32[]{:S(2)}, u32[]{:S(2)}) collective-permute-start(bf16[8,176,128]{2,1,0:T(8,128)(2,1)S(1)} %get-tuple-element.41), channel_id=1, source_target_pairs={{0,1},{1,0},{2,3},{3,2},{4,5},{5,4},{6,7},{7,6},{8,9},{9,8},{10,11... | collective-permute-start | bytes 1081352 | tf_op jit(solution)/shard_map/ppermute | solution.py:85
  112.3 5.8 %collective-permute-start.27 = (bf16[2,176,128]{2,1,0:T(8,128)(2,1)S(1)}, bf16[2,176,128]{2,1,0:T(8,128)(2,1)S(1)}, u32[]{:S(2)}, u32[]{:S(2)}) collective-permute-start(bf16[2,176,128]{2,1,0:T(8,128)(2,1)S(1)} %get-tuple-element.43), channel_id=1, source_target_pairs={{0,2},{1,3},{2,4},{3,5},{4,6},{5,7},{6,0},{7,1},{8,10},{9,11},{10,... | collective-permute-start | bytes 270344 | tf_op jit(solution)/shard_map/ppermute | solution.py:89
  113.5 7.1 %collective-permute-start.28 = (bf16[2,176,128]{2,1,0:T(8,128)(2,1)S(1)}, bf16[2,176,128]{2,1,0:T(8,128)(2,1)S(1)}, u32[]{:S(2)}, u32[]{:S(2)}) collective-permute-start(bf16[2,176,128]{2,1,0:T(8,128)(2,1)S(1)} %get-tuple-element.44), channel_id=1, source_target_pairs={{0,4},{1,5},{2,6},{3,7},{4,0},{5,1},{6,2},{7,3},{8,12},{9,13},{10,... | collective-permute-start | bytes 270344 | tf_op jit(solution)/shard_map/ppermute | solution.py:89
  121.4 5.0 %collective-permute-start.32 = (bf16[2,176,128]{2,1,0:T(8,128)(2,1)S(1)}, bf16[2,176,128]{2,1,0:T(8,128)(2,1)S(1)}, u32[]{:S(2)}, u32[]{:S(2)}) collective-permute-start(bf16[2,176,128]{2,1,0:T(8,128)(2,1)S(1)} %get-tuple-element.48.w0), channel_id=1, source_target_pairs={{0,4},{1,5},{2,6},{3,7},{4,0},{5,1},{6,2},{7,3},{8,12},{9,13},{10,... | collective-permute-start | bytes 270344 | tf_op jit(solution)/shard_map/ppermute | solution.py:89
  123.9 5.1 %collective-permute-start.30 = (bf16[2,176,128]{2,1,0:T(8,128)(2,1)S(1)}, bf16[2,176,128]{2,1,0:T(8,128)(2,1)S(1)}, u32[]{:S(2)}, u32[]{:S(2)}) collective-permute-start(bf16[2,176,128]{2,1,0:T(8,128)(2,1)S(1)} %get-tuple-element.48.w0), channel_id=1, source_target_pairs={{0,2},{1,3},{2,4},{3,5},{4,6},{5,7},{6,0},{7,1},{8,10},{9,11},{10,... | collective-permute-start | bytes 270344 | tf_op jit(solution)/shard_map/ppermute | solution.py:89
  129.1 5.1 %collective-permute-start.33 = (bf16[8,176,128]{2,1,0:T(8,128)(2,1)S(1)}, bf16[8,176,128]{2,1,0:T(8,128)(2,1)S(1)}, u32[]{:S(2)}, u32[]{:S(2)}) collective-permute-start(bf16[8,176,128]{2,1,0:T(8,128)(2,1)S(1)} %pad_maximum_fusion), channel_id=1, source_target_pairs={{0,1},{1,0},{2,3},{3,2},{4,5},{5,4},{6,7},{7,6},{8,9},{9,8},{10,11... | collective-permute-start | bytes 1081352 | tf_op jit(solution)/shard_map/ppermute | solution.py:85
  159.6 6.6 %collective-permute-start.39 = (bf16[80,128]{1,0:T(8,128)(2,1)S(1)}, bf16[80,128]{1,0:T(8,128)(2,1)S(1)}, u32[]{:S(2)}, u32[]{:S(2)}) collective-permute-start(bf16[80,128]{1,0:T(8,128)(2,1)S(1)} %shard_map.175.a), channel_id=1, source_target_pairs={{0,32},{8,40},{16,48},{24,56},{32,0},{40,8},{48,16},{56,24},{64,96... | collective-permute-start | bytes 61448 | tf_op jit(solution)/shard_map/ppermute | solution.py:357
  160.3 5.9 %collective-permute-start.38 = (bf16[80,128]{1,0:T(8,128)(2,1)S(1)}, bf16[80,128]{1,0:T(8,128)(2,1)S(1)}, u32[]{:S(2)}, u32[]{:S(2)}) collective-permute-start(bf16[80,128]{1,0:T(8,128)(2,1)S(1)} %shard_map.175.a), channel_id=1, source_target_pairs={{0,48},{8,56},{16,32},{24,40},{32,16},{40,24},{48,0},{56,8},{64,11... | collective-permute-start | bytes 61448 | tf_op jit(solution)/shard_map/ppermute | solution.py:357
  161.2 5.5 %collective-permute-start.37 = (bf16[80,128]{1,0:T(8,128)(2,1)S(1)}, bf16[80,128]{1,0:T(8,128)(2,1)S(1)}, u32[]{:S(2)}, u32[]{:S(2)}) collective-permute-start(bf16[80,128]{1,0:T(8,128)(2,1)S(1)} %shard_map.175.a), channel_id=1, source_target_pairs={{0,16},{8,24},{16,0},{24,8},{32,48},{40,56},{48,32},{56,40},{64,80... | collective-permute-start | bytes 61448 | tf_op jit(solution)/shard_map/ppermute | solution.py:357
  (18 other events, 330.6 us)
where the time goes:
time: 180 us; the launch traced here: 178 us
  starting transfers between devices  69.6 us (39%)
  waiting for transfers between devices  49.7 us (28%)
  Pallas kernels  31.8 us (18%)
  blocking collectives  22.1 us (12%)
  local copies, waits for them, and re-layouts  2.41 us (1%)
    ppermute x22, waiting for transfers between devices, step(): return lax.ppermute(x, 'row', pairs)  31.3 us
    ppermute x22, starting transfers between devices, step(): return lax.ppermute(x, 'row', pairs)  29.4 us
    all_to_all x2, blocking collectives, sum_everywhere(): x = lax.all_to_all(x, every, 0, 0, tiled=True, axis_index_groups=groups)  22.1 us
    ppermute x3, starting transfers between devices, to_sibling(): return lax.ppermute(x, 'col', [(i, i ^ 1) for i in range(8)])  17.1 us
    ppermute x9, starting transfers between devices, along_x(): return lax.ppermute(x, 'col', [(i, (i + 2 * shift) % 8) for i in range(8)])  14.5 us
    ppermute x9, waiting for transfers between devices, along_x(): return lax.ppermute(x, 'col', [(i, (i + 2 * shift) % 8) for i in range(8)])  11.3 us
    pallas_call x4, Pallas kernels, on_device(): call(functools.partial(degree_kernel, i * GROUP), shape((16, 8, EDGE), F3...  10.3 us
    pallas_call x1, Pallas kernels, on_device(): call(functools.partial(last_kernel, n_feat), shape((1280, EDGE), BF16), [...  9.42 us
  transfers between devices with their start and end apart: 40, of which 26 were waited for; matrix products, arithmetic and copies ran while one was open for 0% of the time, Pallas kernels for 6%

commit v1 on v0

--- a/solution.py
+++ b/solution.py
@@ -170,6 +170,13 @@
     return x.astype(F32).T
 
 
+def weights_kernel(first, bias, self_t, neigh_t, first_t, bias_t, self_second, neigh_second):
+    first_t[...] = flip(first[...]).astype(BF16)
+    bias_t[...] = jnp.broadcast_to(bias[...], (EDGE, bias.shape[1])).T
+    self_second[...] = flip(self_t[...]).astype(BF16)
+    neigh_second[...] = flip(neigh_t[...]).astype(BF16)
+
+
 def aggregate_kernel(s0, s1, s2, s3, agg, inv):
     total = (s0[...] + s1[...]) + (s2[...] + s3[...])
     for b in range(2):
@@ -185,9 +192,9 @@
     feat_parts, agg_parts = refs[:n_parts], refs[n_parts : 2 * n_parts]
     agg, keep, send, mine, held, acc = refs[2 * n_parts :]
     acc[...] = jnp.zeros_like(acc)
-    weights_t = flip(weights[...]).astype(BF16)
+    weights_t = weights[...]
     wide = 4
-    bias_t = jnp.broadcast_to(bias[...], (wide * EDGE, bias.shape[1])).T
+    bias_t = jnp.concatenate([bias[...]] * wide, axis=1)
     first = 0
     for feat_part, agg_part in zip(feat_parts, agg_parts):
 
@@ -252,7 +259,7 @@
 
 
 def last_kernel(
-    n_parts, slots, cols, w0, w1, w2, w3, sibling, held, tiles, agg_second, lg, self_t, neigh_t,
+    n_parts, slots, cols, w0, w1, w2, w3, sibling, held, tiles, agg_second, lg, self_second, neigh_second,
     grad_self, grad_bias, *refs
 ):
     feat_parts, agg_parts = refs[:n_parts], refs[n_parts : 2 * n_parts]
@@ -260,16 +267,14 @@
     copies = start_pairs(feat_parts, agg_parts, both, both_sem)
     acc[...] = jnp.zeros_like(acc)
     lacking = jnp.zeros((256 - PAD, EDGE), BF16)
-    self_second = flip(self_t[...]).astype(BF16)
-    neigh_second = flip(neigh_t[...]).astype(BF16)
     for b in range(2):
-        acc[b] = dot(self_second, jnp.concatenate([lg[b], lacking], axis=0))
+        acc[b] = dot(self_second[...], jnp.concatenate([lg[b], lacking], axis=0))
     g_neigh = jnp.zeros((PAD, 256), F32)
     for i, (dx, part) in enumerate(zip(X_ORDER, (w0, w1, w2, w3))):
         at = [(j // 2 * 4 + dx) * 2 + j % 2 for j in range(4)]
         w = jnp.concatenate([part[0], part[1], sibling[2 * i], sibling[2 * i + 1]], axis=1)
         tall = jnp.concatenate([w, jnp.concatenate([lacking] * 4, axis=1)], axis=0)
-        got = dot(neigh_second, tall).astype(BF16)
+        got = dot(neigh_second[...], tall).astype(BF16)
         for j in range(4):
             proj[at[j]] = got[:, j * EDGE : (j + 1) * EDGE]
         g_neigh += dot_nt(w, jnp.concatenate([agg_second[s] for s in at], axis=1))
@@ -422,12 +427,17 @@
         aggregate_kernel, (shape((2, EDGE, EDGE), BF16), shape((2, EDGE), F32)), [VMEM] * 4
     )(sums[0], along_x(sums[1], 1), along_x(sums[2], 2), along_x(sums[3], 3))
     agg_parts = ring(jnp.concatenate(along_y(agg), axis=0), ALONG_Z)
-    weights = jnp.concatenate([self_first, neigh_first], axis=0)
-    bias = bias_first.reshape(1, -1)
 
     lacking = ((0, 256 - classes), (0, 0))
     self_t = jnp.pad(self_second.T, lacking)
     neigh_t = jnp.pad(neigh_second.T, lacking)
+    square = shape((256, 256), BF16)
+    weights, bias, self_wide, neigh_wide = call(
+        weights_kernel,
+        (square, shape((hid_size, EDGE), F32), square, square),
+        [VMEM] * 4,
+        flops=2**30,
+    )(jnp.concatenate([self_first, neigh_first], axis=0), bias_first.reshape(1, -1), self_t, neigh_t)
     bias_wide = jnp.broadcast_to(jnp.pad(bias_second, (0, PAD - classes))[:, None], (PAD, EDGE))
     half = shape((8, PAD, EDGE), BF16)
     agg_second, keep, send, mine, hid = call(
@@ -485,7 +495,7 @@
         flops=2**31,
         bytes_accessed=2**24,
     )(
-        slots, cols, *w_parts, hid, tiles, agg_second, lg, self_t, neigh_t, grad_self,
+        slots, cols, *w_parts, hid, tiles, agg_second, lg, self_wide, neigh_wide, grad_self,
         grad_bias, *feat_parts, *agg_parts
     )
     out = call(

time: 180 us -> 184 us (1.022)
  starting transfers between devices: 69.6 us -> 73.5 us
    ppermute x22, starting transfers between devices: 29.4 us -> 34.5 us  [step(): return lax.ppermute(x, 'row', pairs)]
    ppermute x22, waiting for transfers between devices: 31.3 us -> 26.9 us  [step(): return lax.ppermute(x, 'row', pairs)]
    ppermute x3, waiting for transfers between devices: 1.46 us -> 4.57 us  [sum_everywhere(): lax.ppermute(x, 'row', [(i, i ^ flip_bits) for i in range(32)])]
  transfers between devices with their start and end apart: 40 -> 40, of which waited for: 26 -> 24; matrix products, arithmetic and copies ran while one was open for 0% -> 0% of each run, Pallas kernels for 6% -> 6%
where the time goes in v1:
time: 184 us; the launch traced here: 183 us
  starting transfers between devices  73.5 us (40%)
  waiting for transfers between devices  50.2 us (27%)
  Pallas kernels  31.8 us (17%)
  blocking collectives  22.4 us (12%)
  local copies, waits for them, and re-layouts  2.41 us (1%)
    ppermute x22, starting transfers between devices, step(): return lax.ppermute(x, 'row', pairs)  34.5 us
    ppermute x22, waiting for transfers between devices, step(): return lax.ppermute(x, 'row', pairs)  26.9 us
    all_to_all x2, blocking collectives, sum_everywhere(): x = lax.all_to_all(x, every, 0, 0, tiled=True, axis_index_groups=groups)  22.4 us
    ppermute x3, starting transfers between devices, to_sibling(): return lax.ppermute(x, 'col', [(i, i ^ 1) for i in range(8)])  15.9 us
    ppermute x9, starting transfers between devices, along_x(): return lax.ppermute(x, 'col', [(i, (i + 2 * shift) % 8) for i in range(8)])  13.4 us
    ppermute x9, waiting for transfers between devices, along_x(): return lax.ppermute(x, 'col', [(i, (i + 2 * shift) % 8) for i in range(8)])  12.8 us
    pallas_call x4, Pallas kernels, on_device(): call(functools.partial(degree_kernel, i * GROUP), shape((16, 8, EDGE), F3...  10.3 us
    pallas_call x1, Pallas kernels, on_device(): call(functools.partial(last_kernel, n_feat), shape((1280, EDGE), BF16), [...  9.29 us
  transfers between devices with their start and end apart: 40, of which 24 were waited for; matrix products, arithmetic and copies ran while one was open for 0% of the time, Pallas kernels for 6%

profile of v1, /device:TPU:1, one launch (start us, length us, event | category | flops | bytes accessed | tf_op | source)
XLA Modules:
  0.0 182.9 jit_solution(7488227727427497205)
XLA Ops:
  6.7 2.7 %collective-permute-done.2 = bf16[2,128,128]{2,1,0:T(8,128)(2,1)S(1)} collective-permute-done((bf16[2,128,128]{2,1,0:T(8,128)(2,1)}, bf16[2,128,128]{2,1,0:T(8,128)(2,1)S(1)}, u32[]{:S(2)}, u32[]{:S(2)}) %collective-permute-start.2) | collective-permute-done | bytes 65568 | tf_op jit(solution)/shard_map/ppermute | solution.py:46
  10.2 5.5 %collective-permute-start.4 = (bf16[8,128,128]{2,1,0:T(8,128)(2,1)S(1)}, bf16[8,128,128]{2,1,0:T(8,128)(2,1)S(1)}, u32[]{:S(2)}, u32[]{:S(2)}) collective-permute-start(bf16[8,128,128]{2,1,0:T(8,128)(2,1)S(1)} %pad_maximum_fusion.1.refs_0_), channel_id=1, source_target_pairs={{0,56},{8,0},{16,8},{24,16},{32,24},{40,32},{48,40},{56,48},{64,12... | collective-permute-start | bytes 786440 | tf_op jit(solution)/shard_map/ppermute | solution.py:46
  17.9 2.6 %shard_map.164.d0 = f32[16,8,128]{2,1,0:T(8,128)S(1)} custom-call(s32[128]{0:T(128)S(1)} %get-tuple-element.69.slots, bf16[128,128,128]{2,1,0:T(8,128)(2,1)S(1)} %bitcast.41), custom_call_target="tpu_custom_call" | custom-call | flops 4294967296 | bytes 1048576 | tf_op jit(solution)/shard_map/pallas_call | solution.py:399
  20.5 2.8 %collective-permute-start.6 = (bf16[8,128,128]{2,1,0:T(8,128)(2,1)S(1)}, bf16[8,128,128]{2,1,0:T(8,128)(2,1)S(1)}, u32[]{:S(2)}, u32[]{:S(2)}) collective-permute-start(bf16[8,128,128]{2,1,0:T(8,128)(2,1)S(1)} %collective-permute-done.4.refs_2_), channel_id=1, source_target_pairs={{0,56},{8,0},{16,8},{24,16},{32,24},{40,32},{48,40},{56,48},{64,12... | collective-permute-start | bytes 786440 | tf_op jit(solution)/shard_map/ppermute | solution.py:46
  23.3 2.6 %shard_map.165.d1 = f32[16,8,128]{2,1,0:T(8,128)S(1)} custom-call(s32[128]{0:T(128)S(1)} %get-tuple-element.69.slots, bf16[128,128,128]{2,1,0:T(8,128)(2,1)S(1)} %bitcast.42), custom_call_target="tpu_custom_call" | custom-call | flops 4294967296 | bytes 1048576 | tf_op jit(solution)/shard_map/pallas_call | solution.py:399
  26.6 3.1 %collective-permute-start.8 = (bf16[8,128,128]{2,1,0:T(8,128)(2,1)S(1)}, bf16[8,128,128]{2,1,0:T(8,128)(2,1)S(1)}, u32[]{:S(2)}, u32[]{:S(2)}) collective-permute-start(bf16[8,128,128]{2,1,0:T(8,128)(2,1)S(1)} %collective-permute-done.6.refs_4_), channel_id=1, source_target_pairs={{0,56},{8,0},{16,8},{24,16},{32,24},{40,32},{48,40},{56,48},{64,12... | collective-permute-start | bytes 786440 | tf_op jit(solution)/shard_map/ppermute | solution.py:46
  29.7 2.6 %shard_map.166.d2 = f32[16,8,128]{2,1,0:T(8,128)S(1)} custom-call(s32[128]{0:T(128)S(1)} %get-tuple-element.69.slots, bf16[128,128,128]{2,1,0:T(8,128)(2,1)S(1)} %bitcast.43), custom_call_target="tpu_custom_call" | custom-call | flops 4294967296 | bytes 1048576 | tf_op jit(solution)/shard_map/pallas_call | solution.py:399
  33.0 3.2 %collective-permute-start.10 = (bf16[4,128,128]{2,1,0:T(8,128)(2,1)S(1)}, bf16[4,128,128]{2,1,0:T(8,128)(2,1)S(1)}, u32[]{:S(2)}, u32[]{:S(2)}) collective-permute-start(bf16[4,128,128]{2,1,0:T(8,128)(2,1)S(1)} %slice.25), channel_id=1, source_target_pairs={{0,56},{8,0},{16,8},{24,16},{32,24},{40,32},{48,40},{56,48},{64,12... | collective-permute-start | bytes 393224 | tf_op jit(solution)/shard_map/ppermute | solution.py:46
  36.3 2.6 %shard_map.167.d3 = f32[16,8,128]{2,1,0:T(8,128)S(1)} custom-call(s32[128]{0:T(128)S(1)} %get-tuple-element.69.slots, bf16[128,128,128]{2,1,0:T(8,128)(2,1)S(1)} %bitcast.44), custom_call_target="tpu_custom_call" | custom-call | flops 4294967296 | bytes 1048576 | tf_op jit(solution)/shard_map/pallas_call | solution.py:399
  38.9 3.3 %collective-permute-done.9.refs_7_ = bf16[4,128,128]{2,1,0:T(8,128)(2,1)S(1)} collective-permute-done((bf16[4,128,128]{2,1,0:T(8,128)(2,1)S(1)}, bf16[4,128,128]{2,1,0:T(8,128)(2,1)S(1)}, u32[]{:S(2)}, u32[]{:S(2)}) %collective-permute-start.9) | collective-permute-done | bytes 131104 | tf_op jit(solution)/shard_map/ppermute | solution.py:46
  42.2 3.3 %shard_map.168 = (f32[1056,128]{1,0:T(8,128)S(1)}, f32[1056,128]{1,0:T(8,128)S(1)}) custom-call(s32[128]{0:T(128)S(1)} %get-tuple-element.68.offs, s32[128]{0:T(128)S(1)} %get-tuple-element.70.cols, bf16[128,128,128]{2,1,0:T(8,128)(2,1)S(1)} %bitcast.45, f32[16,8,128]{2,1,0:T(8,128)S(1)} %shard_map.164.d0, f32[16,8,128]{2,1,0:T(8,128)S(1)} %shard_map.165.d1, ...), custom_call_target="tpu_custom_call" | custom-call | flops 536870912 | bytes 8388608 | tf_op jit(solution)/shard_map/pallas_call | solution.py:410
  45.5 6.5 %collective-permute-start.11 = (f32[1056,128]{1,0:T(8,128)S(1)}, f32[1056,128]{1,0:T(8,128)S(1)}, u32[]{:S(2)}, u32[]{:S(2)}) collective-permute-start(f32[1056,128]{1,0:T(8,128)S(1)} %get-tuple-element.40), channel_id=1, source_target_pairs={{0,1},{1,0},{2,3},{3,2},{4,5},{5,4},{6,7},{7,6},{8,9},{9,8},{10,11... | collective-permute-start | bytes 1622024 | tf_op jit(solution)/shard_map/ppermute | solution.py:85
  54.9 2.5 %collective-permute-start.13 = (f32[264,128]{1,0:T(8,128)S(1)}, f32[264,128]{1,0:T(8,128)S(1)}, u32[]{:S(2)}, u32[]{:S(2)}) collective-permute-start(f32[264,128]{1,0:T(8,128)S(1)} %get-tuple-element.43), channel_id=1, source_target_pairs={{0,4},{1,5},{2,6},{3,7},{4,0},{5,1},{6,2},{7,3},{8,12},{9,13},{10,... | collective-permute-start | bytes 405512 | tf_op jit(solution)/shard_map/ppermute | solution.py:89
  59.7 3.9 %collective-permute-done.13.s2 = f32[264,128]{1,0:T(8,128)S(1)} collective-permute-done((f32[264,128]{1,0:T(8,128)S(1)}, f32[264,128]{1,0:T(8,128)S(1)}, u32[]{:S(2)}, u32[]{:S(2)}) %collective-permute-start.13) | collective-permute-done | bytes 135200 | tf_op jit(solution)/shard_map/ppermute | solution.py:89
  63.8 2.7 %collective-permute-start.16 = (bf16[2,128,128]{2,1,0:T(8,128)(2,1)S(1)}, bf16[2,128,128]{2,1,0:T(8,128)(2,1)S(1)}, u32[]{:S(2)}, u32[]{:S(2)}) collective-permute-start(bf16[2,128,128]{2,1,0:T(8,128)(2,1)S(1)} %get-tuple-element.45), channel_id=1, source_target_pairs={{0,192},{64,0},{128,64},{192,128},{8,200},{72,8},{136,72},{200,136... | collective-permute-start | bytes 196616 | tf_op jit(solution)/shard_map/ppermute | solution.py:46
  68.1 2.9 %collective-permute-done.17 = bf16[2,128,128]{2,1,0:T(8,128)(2,1)S(1)} collective-permute-done((bf16[2,128,128]{2,1,0:T(8,128)(2,1)S(1)}, bf16[2,128,128]{2,1,0:T(8,128)(2,1)S(1)}, u32[]{:S(2)}, u32[]{:S(2)}) %collective-permute-start.17) | collective-permute-done | bytes 65568 | tf_op jit(solution)/shard_map/ppermute | solution.py:46
  71.2 2.7 %collective-permute-start.19 = (bf16[8,128,128]{2,1,0:T(8,128)(2,1)S(1)}, bf16[8,128,128]{2,1,0:T(8,128)(2,1)S(1)}, u32[]{:S(2)}, u32[]{:S(2)}) collective-permute-start(bf16[8,128,128]{2,1,0:T(8,128)(2,1)S(1)} %constant_dynamic-update-slice_fusion.refs_9_), channel_id=1, source_target_pairs={{0,56},{8,0},{16,8},{24,16},{32,24},{40,32},{48,40},{56,48},{64,12... | collective-permute-start | bytes 786440 | tf_op jit(solution)/shard_map/ppermute | solution.py:46
  73.8 3.8 %collective-permute-done.18.refs_10_ = bf16[8,128,128]{2,1,0:T(8,128)(2,1)S(1)} collective-permute-done((bf16[8,128,128]{2,1,0:T(8,128)(2,1)S(1)}, bf16[8,128,128]{2,1,0:T(8,128)(2,1)S(1)}, u32[]{:S(2)}, u32[]{:S(2)}) %collective-permute-start.18) | collective-permute-done | bytes 262176 | tf_op jit(solution)/shard_map/ppermute | solution.py:46
  77.6 2.7 %collective-permute-start.21 = (bf16[8,128,128]{2,1,0:T(8,128)(2,1)S(1)}, bf16[8,128,128]{2,1,0:T(8,128)(2,1)S(1)}, u32[]{:S(2)}, u32[]{:S(2)}) collective-permute-start(bf16[8,128,128]{2,1,0:T(8,128)(2,1)S(1)} %collective-permute-done.19.refs_11_), channel_id=1, source_target_pairs={{0,56},{8,0},{16,8},{24,16},{32,24},{40,32},{48,40},{56,48},{64,12... | collective-permute-start | bytes 786440 | tf_op jit(solution)/shard_map/ppermute | solution.py:46
  80.3 3.8 %collective-permute-done.20.refs_12_ = bf16[8,128,128]{2,1,0:T(8,128)(2,1)S(1)} collective-permute-done((bf16[8,128,128]{2,1,0:T(8,128)(2,1)S(1)}, bf16[8,128,128]{2,1,0:T(8,128)(2,1)S(1)}, u32[]{:S(2)}, u32[]{:S(2)}) %collective-permute-start.20) | collective-permute-done | bytes 262176 | tf_op jit(solution)/shard_map/ppermute | solution.py:46
  84.0 2.7 %collective-permute-start.23 = (bf16[8,128,128]{2,1,0:T(8,128)(2,1)S(1)}, bf16[8,128,128]{2,1,0:T(8,128)(2,1)S(1)}, u32[]{:S(2)}, u32[]{:S(2)}) collective-permute-start(bf16[8,128,128]{2,1,0:T(8,128)(2,1)S(1)} %collective-permute-done.21.refs_13_), channel_id=1, source_target_pairs={{0,56},{8,0},{16,8},{24,16},{32,24},{40,32},{48,40},{56,48},{64,12... | collective-permute-start | bytes 786440 | tf_op jit(solution)/shard_map/ppermute | solution.py:46
  86.7 4.6 %collective-permute-done.22.refs_14_ = bf16[8,128,128]{2,1,0:T(8,128)(2,1)S(1)} collective-permute-done((bf16[8,128,128]{2,1,0:T(8,128)(2,1)S(1)}, bf16[8,128,128]{2,1,0:T(8,128)(2,1)S(1)}, u32[]{:S(2)}, u32[]{:S(2)}) %collective-permute-start.22) | collective-permute-done | bytes 262176 | tf_op jit(solution)/shard_map/ppermute | solution.py:46
  91.5 2.9 %collective-permute-start.25 = (bf16[4,128,128]{2,1,0:T(8,128)(2,1)S(1)}, bf16[4,128,128]{2,1,0:T(8,128)(2,1)S(1)}, u32[]{:S(2)}, u32[]{:S(2)}) collective-permute-start(bf16[4,128,128]{2,1,0:T(8,128)(2,1)S(1)} %slice.27), channel_id=1, source_target_pairs={{0,56},{8,0},{16,8},{24,16},{32,24},{40,32},{48,40},{56,48},{64,12... | collective-permute-start | bytes 393224 | tf_op jit(solution)/shard_map/ppermute | solution.py:46
  94.7 3.5 %collective-permute-done.24.refs_16_ = bf16[4,128,128]{2,1,0:T(8,128)(2,1)S(1)} collective-permute-done((bf16[4,128,128]{2,1,0:T(8,128)(2,1)S(1)}, bf16[4,128,128]{2,1,0:T(8,128)(2,1)S(1)}, u32[]{:S(2)}, u32[]{:S(2)}) %collective-permute-start.24) | collective-permute-done | bytes 131104 | tf_op jit(solution)/shard_map/ppermute | solution.py:46
  98.2 6.9 %shard_map.171 = (bf16[16,256,128]{2,1,0:T(8,128)(2,1)S(1)}, bf16[8,176,128]{2,1,0:T(8,128)(2,1)S(1)}, bf16[8,176,128]{2,1,0:T(8,128)(2,1)S(1)}, bf16[2,256,128]...) custom-call(s32[128]{0:T(128)S(1)} %get-tuple-element.69.slots, s32[128]{0:T(128)S(1)} %get-tuple-element.70.cols, ...), custom_call_target="tpu_custom_call" | custom-call | flops 2147483648 | bytes 8388608 | tf_op jit(solution)/shard_map/pallas_call | solution.py:443
  105.0 7.3 %collective-permute-start.26 = (bf16[8,176,128]{2,1,0:T(8,128)(2,1)S(1)}, bf16[8,176,128]{2,1,0:T(8,128)(2,1)S(1)}, u32[]{:S(2)}, u32[]{:S(2)}) collective-permute-start(bf16[8,176,128]{2,1,0:T(8,128)(2,1)S(1)} %get-tuple-element.47), channel_id=1, source_target_pairs={{0,1},{1,0},{2,3},{3,2},{4,5},{5,4},{6,7},{7,6},{8,9},{9,8},{10,11... | collective-permute-start | bytes 1081352 | tf_op jit(solution)/shard_map/ppermute | solution.py:85
  127.0 3.7 %collective-permute-done.32.w3 = bf16[2,176,128]{2,1,0:T(8,128)(2,1)S(1)} collective-permute-done((bf16[2,176,128]{2,1,0:T(8,128)(2,1)S(1)}, bf16[2,176,128]{2,1,0:T(8,128)(2,1)S(1)}, u32[]{:S(2)}, u32[]{:S(2)}) %collective-permute-start.32) | collective-permute-done | bytes 90144 | tf_op jit(solution)/shard_map/ppermute | solution.py:89
  134.2 9.3 %shard_map.174 = bf16[1280,128]{1,0:T(8,128)(2,1)S(1)} custom-call(s32[128]{0:T(128)S(1)} %get-tuple-element.69.slots, s32[128]{0:T(128)S(1)} %get-tuple-element.70.cols, bf16[2,176,128]{2,1,0:T(8,128)(2,1)S(1)} %get-tuple-element.54.w0, bf16[2,176,128]{2,1,0:T(8,128)(2,1)S(1)} %collective-permute-done.30.w1, ...), custom_call_target="tpu_custom_call" | custom-call | flops 2147483648 | bytes 16777216 | tf_op jit(solution)/shard_map/pallas_call | solution.py:484
  143.5 11.8 %all_to_all.10.x = bf16[16,80,128]{2,1,0:T(8,128)(2,1)S(1)} all-to-all(bf16[16,80,128]{2,1,0:T(8,128)(2,1)S(1)} %bitcast.49), channel_id=1, replica_groups={{0,2,4,6,64,66,68,70,128,130,132,134,192,194,196,198},{1,3,5,7,65,67,69..., dimensions={0} | all-to-all | bytes 655360 | tf_op jit(solution)/shard_map/all_to_all | solution.py:358
  162.4 2.5 %collective-permute-start.38 = (bf16[80,128]{1,0:T(8,128)(2,1)S(1)}, bf16[80,128]{1,0:T(8,128)(2,1)S(1)}, u32[]{:S(2)}, u32[]{:S(2)}) collective-permute-start(bf16[80,128]{1,0:T(8,128)(2,1)S(1)} %shard_map.176.a), channel_id=1, source_target_pairs={{0,48},{8,56},{16,32},{24,40},{32,16},{40,24},{48,0},{56,8},{64,11... | collective-permute-start | bytes 61448 | tf_op jit(solution)/shard_map/ppermute | solution.py:362
  167.4 4.0 %collective-permute-done.39.d = bf16[80,128]{1,0:T(8,128)(2,1)S(1)} collective-permute-done((bf16[80,128]{1,0:T(8,128)(2,1)S(1)}, bf16[80,128]{1,0:T(8,128)(2,1)S(1)}, u32[]{:S(2)}, u32[]{:S(2)}) %collective-permute-start.39) | collective-permute-done | bytes 20512 | tf_op jit(solution)/shard_map/ppermute | solution.py:362
  171.4 10.6 %all_to_all.11 = bf16[16,80,128]{2,1,0:T(8,128)(2,1)S(1)} all-to-all(bf16[16,80,128]{2,1,0:T(8,128)(2,1)S(1)} %shard_map.177), channel_id=1, replica_groups={{0,2,4,6,64,66,68,70,128,130,132,134,192,194,196,198},{1,3,5,7,65,67,69..., dimensions={0} | all-to-all | bytes 655360 | tf_op jit(solution)/shard_map/all_to_all | solution.py:364
  (102 shorter events, 47.0 us)
Async XLA Ops:
  0.6 6.0 %collective-permute-start = (bf16[2,128,128]{2,1,0:T(8,128)(2,1)}, bf16[2,128,128]{2,1,0:T(8,128)(2,1)S(1)}, u32[]{:S(2)}, u32[]{:S(2)}) collective-permute-start(bf16[2,128,128]{2,1,0:T(8,128)(2,1)} %bitcast.55), channel_id=1, source_target_pairs={{0,64},{64,128},{128,192},{192,0},{8,72},{72,136},{136,200},{200,8... | collective-permute-start | bytes 196616 | tf_op jit(solution)/shard_map/ppermute | solution.py:46
  4.4 4.9 %collective-permute-start.2 = (bf16[2,128,128]{2,1,0:T(8,128)(2,1)}, bf16[2,128,128]{2,1,0:T(8,128)(2,1)S(1)}, u32[]{:S(2)}, u32[]{:S(2)}) collective-permute-start(bf16[2,128,128]{2,1,0:T(8,128)(2,1)} %bitcast.57), channel_id=1, source_target_pairs={{0,128},{64,192},{128,0},{192,64},{8,136},{72,200},{136,8},{200,72... | collective-permute-start | bytes 196616 | tf_op jit(solution)/shard_map/ppermute | solution.py:46
  10.2 10.3 %collective-permute-start.4 = (bf16[8,128,128]{2,1,0:T(8,128)(2,1)S(1)}, bf16[8,128,128]{2,1,0:T(8,128)(2,1)S(1)}, u32[]{:S(2)}, u32[]{:S(2)}) collective-permute-start(bf16[8,128,128]{2,1,0:T(8,128)(2,1)S(1)} %pad_maximum_fusion.1.refs_0_), channel_id=1, source_target_pairs={{0,56},{8,0},{16,8},{24,16},{32,24},{40,32},{48,40},{56,48},{64,12... | collective-permute-start | bytes 786440 | tf_op jit(solution)/shard_map/ppermute | solution.py:46
  15.7 7.5 %collective-permute-start.3 = (bf16[8,128,128]{2,1,0:T(8,128)(2,1)S(1)}, bf16[8,128,128]{2,1,0:T(8,128)(2,1)S(1)}, u32[]{:S(2)}, u32[]{:S(2)}) collective-permute-start(bf16[8,128,128]{2,1,0:T(8,128)(2,1)S(1)} %pad_maximum_fusion.1.refs_0_), channel_id=1, source_target_pairs={{0,8},{8,16},{16,24},{24,32},{32,40},{40,48},{48,56},{56,0},{64,72... | collective-permute-start | bytes 786440 | tf_op jit(solution)/shard_map/ppermute | solution.py:46
  20.5 6.1 %collective-permute-start.6 = (bf16[8,128,128]{2,1,0:T(8,128)(2,1)S(1)}, bf16[8,128,128]{2,1,0:T(8,128)(2,1)S(1)}, u32[]{:S(2)}, u32[]{:S(2)}) collective-permute-start(bf16[8,128,128]{2,1,0:T(8,128)(2,1)S(1)} %collective-permute-done.4.refs_2_), channel_id=1, source_target_pairs={{0,56},{8,0},{16,8},{24,16},{32,24},{40,32},{48,40},{56,48},{64,12... | collective-permute-start | bytes 786440 | tf_op jit(solution)/shard_map/ppermute | solution.py:46
  23.3 6.4 %collective-permute-start.5 = (bf16[8,128,128]{2,1,0:T(8,128)(2,1)S(1)}, bf16[8,128,128]{2,1,0:T(8,128)(2,1)S(1)}, u32[]{:S(2)}, u32[]{:S(2)}) collective-permute-start(bf16[8,128,128]{2,1,0:T(8,128)(2,1)S(1)} %collective-permute-done.3.refs_1_), channel_id=1, source_target_pairs={{0,8},{8,16},{16,24},{24,32},{32,40},{40,48},{48,56},{56,0},{64,72... | collective-permute-start | bytes 786440 | tf_op jit(solution)/shard_map/ppermute | solution.py:46
  26.6 6.4 %collective-permute-start.8 = (bf16[8,128,128]{2,1,0:T(8,128)(2,1)S(1)}, bf16[8,128,128]{2,1,0:T(8,128)(2,1)S(1)}, u32[]{:S(2)}, u32[]{:S(2)}) collective-permute-start(bf16[8,128,128]{2,1,0:T(8,128)(2,1)S(1)} %collective-permute-done.6.refs_4_), channel_id=1, source_target_pairs={{0,56},{8,0},{16,8},{24,16},{32,24},{40,32},{48,40},{56,48},{64,12... | collective-permute-start | bytes 786440 | tf_op jit(solution)/shard_map/ppermute | solution.py:46
  29.7 6.5 %collective-permute-start.7 = (bf16[8,128,128]{2,1,0:T(8,128)(2,1)S(1)}, bf16[8,128,128]{2,1,0:T(8,128)(2,1)S(1)}, u32[]{:S(2)}, u32[]{:S(2)}) collective-permute-start(bf16[8,128,128]{2,1,0:T(8,128)(2,1)S(1)} %collective-permute-done.5.refs_3_), channel_id=1, source_target_pairs={{0,8},{8,16},{16,24},{24,32},{32,40},{40,48},{48,56},{56,0},{64,72... | collective-permute-start | bytes 786440 | tf_op jit(solution)/shard_map/ppermute | solution.py:46
  33.0 5.9 %collective-permute-start.10 = (bf16[4,128,128]{2,1,0:T(8,128)(2,1)S(1)}, bf16[4,128,128]{2,1,0:T(8,128)(2,1)S(1)}, u32[]{:S(2)}, u32[]{:S(2)}) collective-permute-start(bf16[4,128,128]{2,1,0:T(8,128)(2,1)S(1)} %slice.25), channel_id=1, source_target_pairs={{0,56},{8,0},{16,8},{24,16},{32,24},{40,32},{48,40},{56,48},{64,12... | collective-permute-start | bytes 393224 | tf_op jit(solution)/shard_map/ppermute | solution.py:46
  36.2 6.0 %collective-permute-start.9 = (bf16[4,128,128]{2,1,0:T(8,128)(2,1)S(1)}, bf16[4,128,128]{2,1,0:T(8,128)(2,1)S(1)}, u32[]{:S(2)}, u32[]{:S(2)}) collective-permute-start(bf16[4,128,128]{2,1,0:T(8,128)(2,1)S(1)} %slice.24), channel_id=1, source_target_pairs={{0,8},{8,16},{16,24},{24,32},{32,40},{40,48},{48,56},{56,0},{64,72... | collective-permute-start | bytes 393224 | tf_op jit(solution)/shard_map/ppermute | solution.py:46
  45.5 8.0 %collective-permute-start.11 = (f32[1056,128]{1,0:T(8,128)S(1)}, f32[1056,128]{1,0:T(8,128)S(1)}, u32[]{:S(2)}, u32[]{:S(2)}) collective-permute-start(f32[1056,128]{1,0:T(8,128)S(1)} %get-tuple-element.40), channel_id=1, source_target_pairs={{0,1},{1,0},{2,3},{3,2},{4,5},{5,4},{6,7},{7,6},{8,9},{9,8},{10,11... | collective-permute-start | bytes 1622024 | tf_op jit(solution)/shard_map/ppermute | solution.py:85
  53.6 6.1 %collective-permute-start.12 = (f32[264,128]{1,0:T(8,128)S(1)}, f32[264,128]{1,0:T(8,128)S(1)}, u32[]{:S(2)}, u32[]{:S(2)}) collective-permute-start(f32[264,128]{1,0:T(8,128)S(1)} %get-tuple-element.42), channel_id=1, source_target_pairs={{0,2},{1,3},{2,4},{3,5},{4,6},{5,7},{6,0},{7,1},{8,10},{9,11},{10,... | collective-permute-start | bytes 405512 | tf_op jit(solution)/shard_map/ppermute | solution.py:89
  54.9 8.7 %collective-permute-start.13 = (f32[264,128]{1,0:T(8,128)S(1)}, f32[264,128]{1,0:T(8,128)S(1)}, u32[]{:S(2)}, u32[]{:S(2)}) collective-permute-start(f32[264,128]{1,0:T(8,128)S(1)} %get-tuple-element.43), channel_id=1, source_target_pairs={{0,4},{1,5},{2,6},{3,7},{4,0},{5,1},{6,2},{7,3},{8,12},{9,13},{10,... | collective-permute-start | bytes 405512 | tf_op jit(solution)/shard_map/ppermute | solution.py:89
  57.3 6.2 %collective-permute-start.14 = (f32[264,128]{1,0:T(8,128)S(1)}, f32[264,128]{1,0:T(8,128)S(1)}, u32[]{:S(2)}, u32[]{:S(2)}) collective-permute-start(f32[264,128]{1,0:T(8,128)S(1)} %get-tuple-element.44), channel_id=1, source_target_pairs={{0,6},{1,7},{2,0},{3,1},{4,2},{5,3},{6,4},{7,5},{8,14},{9,15},{10,... | collective-permute-start | bytes 405512 | tf_op jit(solution)/shard_map/ppermute | solution.py:89
  66.4 4.6 %collective-permute-start.17 = (bf16[2,128,128]{2,1,0:T(8,128)(2,1)S(1)}, bf16[2,128,128]{2,1,0:T(8,128)(2,1)S(1)}, u32[]{:S(2)}, u32[]{:S(2)}) collective-permute-start(bf16[2,128,128]{2,1,0:T(8,128)(2,1)S(1)} %get-tuple-element.45), channel_id=1, source_target_pairs={{0,128},{64,192},{128,0},{192,64},{8,136},{72,200},{136,8},{200,72... | collective-permute-start | bytes 196616 | tf_op jit(solution)/shard_map/ppermute | solution.py:46
  71.1 6.5 %collective-permute-start.18 = (bf16[8,128,128]{2,1,0:T(8,128)(2,1)S(1)}, bf16[8,128,128]{2,1,0:T(8,128)(2,1)S(1)}, u32[]{:S(2)}, u32[]{:S(2)}) collective-permute-start(bf16[8,128,128]{2,1,0:T(8,128)(2,1)S(1)} %constant_dynamic-update-slice_fusion.refs_9_), channel_id=1, source_target_pairs={{0,8},{8,16},{16,24},{24,32},{32,40},{40,48},{48,56},{56,0},{64,72... | collective-permute-start | bytes 786440 | tf_op jit(solution)/shard_map/ppermute | solution.py:46
  71.2 6.4 %collective-permute-start.19 = (bf16[8,128,128]{2,1,0:T(8,128)(2,1)S(1)}, bf16[8,128,128]{2,1,0:T(8,128)(2,1)S(1)}, u32[]{:S(2)}, u32[]{:S(2)}) collective-permute-start(bf16[8,128,128]{2,1,0:T(8,128)(2,1)S(1)} %constant_dynamic-update-slice_fusion.refs_9_), channel_id=1, source_target_pairs={{0,56},{8,0},{16,8},{24,16},{32,24},{40,32},{48,40},{56,48},{64,12... | collective-permute-start | bytes 786440 | tf_op jit(solution)/shard_map/ppermute | solution.py:46
  77.6 6.4 %collective-permute-start.20 = (bf16[8,128,128]{2,1,0:T(8,128)(2,1)S(1)}, bf16[8,128,128]{2,1,0:T(8,128)(2,1)S(1)}, u32[]{:S(2)}, u32[]{:S(2)}) collective-permute-start(bf16[8,128,128]{2,1,0:T(8,128)(2,1)S(1)} %collective-permute-done.18.refs_10_), channel_id=1, source_target_pairs={{0,8},{8,16},{16,24},{24,32},{32,40},{40,48},{48,56},{56,0},{64,72... | collective-permute-start | bytes 786440 | tf_op jit(solution)/shard_map/ppermute | solution.py:46
  77.6 6.4 %collective-permute-start.21 = (bf16[8,128,128]{2,1,0:T(8,128)(2,1)S(1)}, bf16[8,128,128]{2,1,0:T(8,128)(2,1)S(1)}, u32[]{:S(2)}, u32[]{:S(2)}) collective-permute-start(bf16[8,128,128]{2,1,0:T(8,128)(2,1)S(1)} %collective-permute-done.19.refs_11_), channel_id=1, source_target_pairs={{0,56},{8,0},{16,8},{24,16},{32,24},{40,32},{48,40},{56,48},{64,12... | collective-permute-start | bytes 786440 | tf_op jit(solution)/shard_map/ppermute | solution.py:46
  84.0 7.3 %collective-permute-start.22 = (bf16[8,128,128]{2,1,0:T(8,128)(2,1)S(1)}, bf16[8,128,128]{2,1,0:T(8,128)(2,1)S(1)}, u32[]{:S(2)}, u32[]{:S(2)}) collective-permute-start(bf16[8,128,128]{2,1,0:T(8,128)(2,1)S(1)} %collective-permute-done.20.refs_12_), channel_id=1, source_target_pairs={{0,8},{8,16},{16,24},{24,32},{32,40},{40,48},{48,56},{56,0},{64,72... | collective-permute-start | bytes 786440 | tf_op jit(solution)/shard_map/ppermute | solution.py:46
  84.0 7.4 %collective-permute-start.23 = (bf16[8,128,128]{2,1,0:T(8,128)(2,1)S(1)}, bf16[8,128,128]{2,1,0:T(8,128)(2,1)S(1)}, u32[]{:S(2)}, u32[]{:S(2)}) collective-permute-start(bf16[8,128,128]{2,1,0:T(8,128)(2,1)S(1)} %collective-permute-done.21.refs_13_), channel_id=1, source_target_pairs={{0,56},{8,0},{16,8},{24,16},{32,24},{40,32},{48,40},{56,48},{64,12... | collective-permute-start | bytes 786440 | tf_op jit(solution)/shard_map/ppermute | solution.py:46
  91.4 6.8 %collective-permute-start.24 = (bf16[4,128,128]{2,1,0:T(8,128)(2,1)S(1)}, bf16[4,128,128]{2,1,0:T(8,128)(2,1)S(1)}, u32[]{:S(2)}, u32[]{:S(2)}) collective-permute-start(bf16[4,128,128]{2,1,0:T(8,128)(2,1)S(1)} %slice.26), channel_id=1, source_target_pairs={{0,8},{8,16},{16,24},{24,32},{32,40},{40,48},{48,56},{56,0},{64,72... | collective-permute-start | bytes 393224 | tf_op jit(solution)/shard_map/ppermute | solution.py:46
  91.5 6.7 %collective-permute-start.25 = (bf16[4,128,128]{2,1,0:T(8,128)(2,1)S(1)}, bf16[4,128,128]{2,1,0:T(8,128)(2,1)S(1)}, u32[]{:S(2)}, u32[]{:S(2)}) collective-permute-start(bf16[4,128,128]{2,1,0:T(8,128)(2,1)S(1)} %slice.27), channel_id=1, source_target_pairs={{0,56},{8,0},{16,8},{24,16},{32,24},{40,32},{48,40},{56,48},{64,12... | collective-permute-start | bytes 393224 | tf_op jit(solution)/shard_map/ppermute | solution.py:46
  105.0 8.6 %collective-permute-start.26 = (bf16[8,176,128]{2,1,0:T(8,128)(2,1)S(1)}, bf16[8,176,128]{2,1,0:T(8,128)(2,1)S(1)}, u32[]{:S(2)}, u32[]{:S(2)}) collective-permute-start(bf16[8,176,128]{2,1,0:T(8,128)(2,1)S(1)} %get-tuple-element.47), channel_id=1, source_target_pairs={{0,1},{1,0},{2,3},{3,2},{4,5},{5,4},{6,7},{7,6},{8,9},{9,8},{10,11... | collective-permute-start | bytes 1081352 | tf_op jit(solution)/shard_map/ppermute | solution.py:85
  113.7 5.1 %collective-permute-start.27 = (bf16[2,176,128]{2,1,0:T(8,128)(2,1)S(1)}, bf16[2,176,128]{2,1,0:T(8,128)(2,1)S(1)}, u32[]{:S(2)}, u32[]{:S(2)}) collective-permute-start(bf16[2,176,128]{2,1,0:T(8,128)(2,1)S(1)} %get-tuple-element.49), channel_id=1, source_target_pairs={{0,2},{1,3},{2,4},{3,5},{4,6},{5,7},{6,0},{7,1},{8,10},{9,11},{10,... | collective-permute-start | bytes 270344 | tf_op jit(solution)/shard_map/ppermute | solution.py:89
  114.8 6.3 %collective-permute-start.28 = (bf16[2,176,128]{2,1,0:T(8,128)(2,1)S(1)}, bf16[2,176,128]{2,1,0:T(8,128)(2,1)S(1)}, u32[]{:S(2)}, u32[]{:S(2)}) collective-permute-start(bf16[2,176,128]{2,1,0:T(8,128)(2,1)S(1)} %get-tuple-element.50), channel_id=1, source_target_pairs={{0,4},{1,5},{2,6},{3,7},{4,0},{5,1},{6,2},{7,3},{8,12},{9,13},{10,... | collective-permute-start | bytes 270344 | tf_op jit(solution)/shard_map/ppermute | solution.py:89
  116.9 4.6 %collective-permute-start.29 = (bf16[2,176,128]{2,1,0:T(8,128)(2,1)S(1)}, bf16[2,176,128]{2,1,0:T(8,128)(2,1)S(1)}, u32[]{:S(2)}, u32[]{:S(2)}) collective-permute-start(bf16[2,176,128]{2,1,0:T(8,128)(2,1)S(1)} %get-tuple-element.51), channel_id=1, source_target_pairs={{0,6},{1,7},{2,0},{3,1},{4,2},{5,3},{6,4},{7,5},{8,14},{9,15},{10,... | collective-permute-start | bytes 270344 | tf_op jit(solution)/shard_map/ppermute | solution.py:89
  122.3 4.7 %collective-permute-start.30 = (bf16[2,176,128]{2,1,0:T(8,128)(2,1)S(1)}, bf16[2,176,128]{2,1,0:T(8,128)(2,1)S(1)}, u32[]{:S(2)}, u32[]{:S(2)}) collective-permute-start(bf16[2,176,128]{2,1,0:T(8,128)(2,1)S(1)} %get-tuple-element.54.w0), channel_id=1, source_target_pairs={{0,2},{1,3},{2,4},{3,5},{4,6},{5,7},{6,0},{7,1},{8,10},{9,11},{10,... | collective-permute-start | bytes 270344 | tf_op jit(solution)/shard_map/ppermute | solution.py:89
  125.1 5.6 %collective-permute-start.32 = (bf16[2,176,128]{2,1,0:T(8,128)(2,1)S(1)}, bf16[2,176,128]{2,1,0:T(8,128)(2,1)S(1)}, u32[]{:S(2)}, u32[]{:S(2)}) collective-permute-start(bf16[2,176,128]{2,1,0:T(8,128)(2,1)S(1)} %get-tuple-element.54.w0), channel_id=1, source_target_pairs={{0,4},{1,5},{2,6},{3,7},{4,0},{5,1},{6,2},{7,3},{8,12},{9,13},{10,... | collective-permute-start | bytes 270344 | tf_op jit(solution)/shard_map/ppermute | solution.py:89
  160.5 6.4 %collective-permute-start.37 = (bf16[80,128]{1,0:T(8,128)(2,1)S(1)}, bf16[80,128]{1,0:T(8,128)(2,1)S(1)}, u32[]{:S(2)}, u32[]{:S(2)}) collective-permute-start(bf16[80,128]{1,0:T(8,128)(2,1)S(1)} %shard_map.176.a), channel_id=1, source_target_pairs={{0,16},{8,24},{16,0},{24,8},{32,48},{40,56},{48,32},{56,40},{64,80... | collective-permute-start | bytes 61448 | tf_op jit(solution)/shard_map/ppermute | solution.py:362
  162.4 5.0 %collective-permute-start.38 = (bf16[80,128]{1,0:T(8,128)(2,1)S(1)}, bf16[80,128]{1,0:T(8,128)(2,1)S(1)}, u32[]{:S(2)}, u32[]{:S(2)}) collective-permute-start(bf16[80,128]{1,0:T(8,128)(2,1)S(1)} %shard_map.176.a), channel_id=1, source_target_pairs={{0,48},{8,56},{16,32},{24,40},{32,16},{40,24},{48,0},{56,8},{64,11... | collective-permute-start | bytes 61448 | tf_op jit(solution)/shard_map/ppermute | solution.py:362
  164.9 6.6 %collective-permute-start.39 = (bf16[80,128]{1,0:T(8,128)(2,1)S(1)}, bf16[80,128]{1,0:T(8,128)(2,1)S(1)}, u32[]{:S(2)}, u32[]{:S(2)}) collective-permute-start(bf16[80,128]{1,0:T(8,128)(2,1)S(1)} %shard_map.176.a), channel_id=1, source_target_pairs={{0,32},{8,40},{16,48},{24,56},{32,0},{40,8},{48,16},{56,24},{64,96... | collective-permute-start | bytes 61448 | tf_op jit(solution)/shard_map/ppermute | solution.py:362
  (18 other events, 370.1 us)
